TPU v7x, 256 devices: a whole 4x4x8 slice. The times are simulated.
256 devices in a mesh: gx: 16 (over z, core), gy: 8 (over y_hi, x), ga: 2 (over y_lo).
Axes of the slice: x: 4, y: 4 (y_hi: 2, y_lo: 2; y = y_hi * 2 + y_lo), z: 8, core: 2. Of those that a mesh axis runs over, the one named last changes fastest.
Arguments:
- euler_table: float32 [3, 2048], replicated, may hold values from -3.140625 to 3.140625
- crystal: float32 [21], replicated, may hold values from -0.08 to 3.4
- orient: int32 [32, 16, 8, 4096], P('ga', 'gx', 'gy'), may hold values from 0 to 2047
- weight: bfloat16 [32, 16, 8, 4096], P('ga', 'gx', 'gy'), may hold values from 0.099609375 to 1
- cell_map: int32 [16, 8, 4096], P('gx', 'gy'), may hold values from 0 to 4095, each once within a row
- density: float32 [256, 128, 16], P('gx', 'gy', 'ga'), may hold values from 0.5 to 2
- velocity: float32 [3, 256, 128, 16], P(None, 'gx', 'gy', 'ga'), may hold values from -6 to 6
- stress: float32 [6, 256, 128, 16], P(None, 'gx', 'gy', 'ga'), may hold values from -6 to 6
Outputs:
- stiffness: float32 [21, 256, 128, 16], P(None, 'gx', 'gy', 'ga')
- final_velocity: float32 [3, 256, 128, 16], P(None, 'gx', 'gy', 'ga')
- final_stress: float32 [6, 256, 128, 16], P(None, 'gx', 'gy', 'ga')
Inputs may be any that keep to these rules, and one draw needn't show every extreme that they name: `cell_map`: each partition's row is a permutation of the 4096 canonical indices.
All inputs are finite; a program needn't handle non-finite values.
Results may differ from a plain program's by a relative error of at most 0.0003.
Values sent between devices are 32-bit elements; how exact they have to be, the bound alone decides.
A program may use at most 128 MiB of HBM per device.

v0:
```python
import jax
import jax.numpy as jnp
from jax import lax
from jax.sharding import PartitionSpec as P

STEPS = 2


stencil_weights = (0.8, -0.2, 4.0 / 105.0, -1.0 / 280.0)
time_step = 0.2
grain_block = 4
voigt_pairs = ((0, 0), (1, 1), (2, 2), (1, 2), (0, 2), (0, 1))
upper_pairs = [
    (row_index, col_index) for row_index in range(6) for col_index in range(row_index, 6)
]


def with_halo(cells, sides, width):
    for axis, dim in sides:
        count = lax.axis_size(axis)
        ends = count - 1
        head = lax.slice_in_dim(cells, 0, width, axis=dim)
        tail = lax.slice_in_dim(cells, cells.shape[dim] - width, cells.shape[dim], axis=dim)
        cells = jnp.concatenate(
            [
                lax.ppermute(tail, axis, [(i, (i + 1) % count) for i in range(ends)]),
                cells,
                lax.ppermute(head, axis, [((i + 1) % count, i) for i in range(ends)]),
            ],
            axis=dim,
        )
    return cells


def symmetric_index(first_index, second_index):
    return upper_pairs.index((min(first_index, second_index), max(first_index, second_index)))


def ordered_sum(summands):
    running = summands[0]
    for summand in summands[1:]:
        running = running + summand
    return running


def rotated_table(euler_table, crystal):
    cos_one, sin_one = (jnp.cos(euler_table[0]), jnp.sin(euler_table[0]))
    cos_mid, sin_mid = (jnp.cos(euler_table[1]), jnp.sin(euler_table[1]))
    cos_two, sin_two = (jnp.cos(euler_table[2]), jnp.sin(euler_table[2]))
    bunge = [
        [
            cos_one * cos_two - sin_one * sin_two * cos_mid,
            sin_one * cos_two + cos_one * sin_two * cos_mid,
            sin_two * sin_mid,
        ],
        [
            -cos_one * sin_two - sin_one * cos_two * cos_mid,
            -sin_one * sin_two + cos_one * cos_two * cos_mid,
            cos_two * sin_mid,
        ],
        [sin_one * sin_mid, -cos_one * sin_mid, cos_mid],
    ]
    rotation = [[bunge[col_index][row_index] for col_index in range(3)] for row_index in range(3)]
    bond = []
    for out_index in range(6):
        first, second = voigt_pairs[out_index]
        bond_row = []
        for in_index in range(6):
            third, fourth = voigt_pairs[in_index]
            if in_index < 3:
                bond_row.append(rotation[first][third] * rotation[second][third])
            else:
                bond_row.append(
                    rotation[first][third] * rotation[second][fourth]
                    + rotation[first][fourth] * rotation[second][third]
                )
        bond.append(bond_row)
    entries = [
        [crystal[symmetric_index(row_index, col_index)] for col_index in range(6)]
        for row_index in range(6)
    ]
    product = [
        [
            ordered_sum([bond[row_index][inner] * entries[inner][col_index] for inner in range(6)])
            for col_index in range(6)
        ]
        for row_index in range(6)
    ]
    rotated = [
        ordered_sum([product[row_index][inner] * bond[col_index][inner] for inner in range(6)])
        for row_index, col_index in upper_pairs
    ]
    return jnp.stack(rotated)


def accumulate(table, orient_rows, weight_rows):
    blocks = orient_rows.shape[0] // grain_block
    count_cells = orient_rows.shape[1]

    def absorb(carry, inputs):
        chosen, masses = inputs
        picked = jnp.take(table, chosen, axis=1)
        masses_wide = masses.astype(jnp.float32)
        return (
            (
                carry[0] + jnp.sum(picked * masses_wide[None], axis=1),
                carry[1] + jnp.sum(masses_wide, axis=0),
            ),
            None,
        )

    initial = (jnp.zeros((21, count_cells), jnp.float32), jnp.zeros((count_cells,), jnp.float32))
    result, unused = lax.scan(
        absorb,
        initial,
        (
            orient_rows.reshape(blocks, grain_block, count_cells),
            weight_rows.reshape(blocks, grain_block, count_cells),
        ),
    )
    return result


def derivative(padded, direction):
    interior = [padded.shape[0]] + [extent - 8 for extent in padded.shape[1:]]

    def window(offset):
        starts = [0, 4, 4, 4]
        starts[direction] = 4 + offset
        return lax.slice(
            padded, starts, [begin + extent for begin, extent in zip(starts, interior)]
        )

    result = stencil_weights[0] * (window(1) - window(-1))
    for order_index in range(1, 4):
        result = result + stencil_weights[order_index] * (
            window(order_index + 1) - window(-order_index - 1)
        )
    return result


def advance_velocity(velocity, padded_stress, density):
    along_x = derivative(jnp.stack([padded_stress[0], padded_stress[5], padded_stress[4]]), 1)
    along_y = derivative(jnp.stack([padded_stress[5], padded_stress[1], padded_stress[3]]), 2)
    along_z = derivative(jnp.stack([padded_stress[4], padded_stress[3], padded_stress[2]]), 3)
    return velocity + time_step * (along_x + along_y + along_z) / density[None]


def advance_stress(stress, padded_velocity, stiffness):
    grad_x = derivative(padded_velocity, 1)
    grad_y = derivative(padded_velocity, 2)
    grad_z = derivative(padded_velocity, 3)
    strain = [
        grad_x[0],
        grad_y[1],
        grad_z[2],
        grad_y[2] + grad_z[1],
        grad_x[2] + grad_z[0],
        grad_x[1] + grad_y[0],
    ]
    updated = []
    for row_index in range(6):
        change = ordered_sum(
            [
                stiffness[symmetric_index(row_index, col_index)] * strain[col_index]
                for col_index in range(6)
            ]
        )
        updated.append(stress[row_index] + time_step * change)
    return jnp.stack(updated)


def on_device(euler_table, crystal, orient, weight, cell_map, density, velocity, stress):
    part_x = lax.axis_size("gx")
    part_y = lax.axis_size("gy")
    layers = lax.axis_size("ga")
    brick_x, brick_y, brick_z = (stress.shape[1], stress.shape[2], stress.shape[3])
    sub_x = brick_x // part_x
    sub_y = brick_y // part_y
    depth = brick_z * layers
    grains = orient.shape[0]
    count_cells = orient.shape[3]
    table = rotated_table(euler_table, crystal)
    summed, total = accumulate(
        table, orient.reshape(grains, count_cells), weight.reshape(grains, count_cells)
    )
    slots = cell_map.reshape(count_cells)
    placed = jnp.zeros((21, count_cells), jnp.float32).at[:, slots].set(summed)
    counted = jnp.zeros((count_cells,), jnp.float32).at[slots].set(total)
    placed = placed.reshape(21, part_x, sub_x, part_y, sub_y, depth)
    counted = counted.reshape(part_x, sub_x, part_y, sub_y, depth)
    placed, counted = (
        lax.psum_scatter(placed, "ga", scatter_dimension=5, tiled=True),
        lax.psum_scatter(counted, "ga", scatter_dimension=4, tiled=True),
    )
    averaged = placed / counted[None]
    moved = lax.all_to_all(
        lax.all_to_all(averaged, "gx", split_axis=1, concat_axis=1, tiled=True),
        "gy",
        split_axis=3,
        concat_axis=3,
        tiled=True,
    )
    stiffness = moved.reshape(21, brick_x, brick_y, brick_z)
    for step_index in range(STEPS):
        padded_stress = with_halo(stress, (("gx", 1), ("gy", 2), ("ga", 3)), 4)
        velocity = advance_velocity(velocity, padded_stress, density)
        padded_velocity = with_halo(velocity, (("gx", 1), ("gy", 2), ("ga", 3)), 4)
        stress = advance_stress(stress, padded_velocity, stiffness)
    return (stiffness, velocity, stress)


def solution(mesh):
    return jax.shard_map(
        on_device,
        mesh=mesh,
        in_specs=(
            P(),
            P(),
            P("ga", "gx", "gy", None),
            P("ga", "gx", "gy", None),
            P("gx", "gy", None),
            P("gx", "gy", "ga"),
            P(None, "gx", "gy", "ga"),
            P(None, "gx", "gy", "ga"),
        ),
        out_specs=(P(None, "gx", "gy", "ga"), P(None, "gx", "gy", "ga"), P(None, "gx", "gy", "ga")),
        check_vma=False,
    )
```

profile of v0, /device:TPU:152, one launch (start us, length us, event | category | flops | bytes accessed | tf_op | source)
XLA Modules:
  0.0 715.3 jit_solution(7120864388756211300)
XLA Ops:
  10.7 4.9 collective-permute-start.1
  16.9 14.1 %multiply_add_fusion = (f32[1,2048]{1,0:T(1,128)S(1)}, f32[1,2048]{1,0:T(1,128)S(1)}, f32[1,2048]{1,0:T(1,128)S(1)}, f32[1,2048]{1,0:T(1,128)S(1)}, f32[1,2048]{...) fusion(f32[]{:T(128)} %bitcast.22, f32[]{:T(128)} %bitcast.21, ...), kind=kLoop, calls=%fused_computation.235 | loop fusion | flops 219136 | bytes 131156 | tf_op jit(solution)/shard_map/add | solution.py:42
  31.0 13.9 %multiply_add_fusion.1 = (f32[1,2048]{1,0:T(1,128)S(1)}, f32[1,2048]{1,0:T(1,128)S(1)}, f32[1,2048]{1,0:T(1,128)S(1)}, f32[1,2048]{1,0:T(1,128)S(1)}, f32[1,2048...) fusion(f32[1,2048]{1,0:T(1,128)S(1)} %get-tuple-element.120, ...), kind=kLoop, calls=%fused_computation.236 | loop fusion | flops 186368 | bytes 163924 | tf_op jit(solution)/shard_map/add | solution.py:42
  44.9 13.6 %multiply_add_fusion.18 = (f32[1,2048]{1,0:T(1,128)S(1)}, f32[1,2048]{1,0:T(1,128)S(1)}, f32[1,2048]{1,0:T(1,128)S(1)}, f32[1,2048]{1,0:T(1,128)S(1)}, f32[1,204...) fusion(f32[1,2048]{1,0:T(1,128)S(1)} %get-tuple-element.120, ...), kind=kLoop, calls=%fused_computation.253 | loop fusion | flops 174080 | bytes 139348 | tf_op jit(solution)/shard_map/add | solution.py:42
  58.5 13.7 %multiply_add_fusion.9 = (f32[1,2048]{1,0:T(1,128)S(1)}, f32[1,2048]{1,0:T(1,128)S(1)}, f32[1,2048]{1,0:T(1,128)S(1)}, f32[1,2048]{1,0:T(1,128)S(1)}, f32[1,2048...) fusion(f32[1,2048]{1,0:T(1,128)S(1)} %get-tuple-element.120, f32[1,2048]{1,0:T(1,128)S(1)} %get-tuple-element.119, ...), kind=kLoop, calls=%fused_computation.244 | loop fusion | flops 182272 | bytes 155732 | tf_op jit(solution)/shard_map/add | solution.py:42
  72.2 13.4 %multiply_add_fusion.28 = (f32[1,2048]{1,0:T(1,128)S(1)}, f32[1,2048]{1,0:T(1,128)S(1)}, f32[1,2048]{1,0:T(1,128)S(1)}, f32[1,2048]{1,0:T(1,128)S(1)}, f32[1,204...) fusion(f32[1,2048]{1,0:T(1,128)S(1)} %get-tuple-element.120, ...), kind=kLoop, calls=%fused_computation.263 | loop fusion | flops 174080 | bytes 155732 | tf_op jit(solution)/shard_map/add | solution.py:42
  85.6 13.4 %multiply_add_fusion.2 = f32[1,2048]{1,0:T(1,128)S(1)} fusion(f32[1,2048]{1,0:T(1,128)S(1)} %get-tuple-element.133, f32[1,2048]{1,0:T(1,128)S(1)} %get-tuple-element.132, f32[1,2048]{1,0:T(1,128)S(1)} %get-tuple-element.131, f32[1,2048]{1,0:T(1,128)S(1)} %get-tuple-element.130, f32[1,2048]{1,0:T(1,128)S(1)} %get-tuple-element.129, ...), kind=kLoop, calls=%fused_computation.237 | loop fusion | flops 157696 | bytes 57428 | tf_op jit(solution)/shard_map/add | solution.py:42
  99.0 13.4 %multiply_add_fusion.10 = f32[1,2048]{1,0:T(1,128)S(1)} fusion(f32[1,2048]{1,0:T(1,128)S(1)} %get-tuple-element.133, f32[1,2048]{1,0:T(1,128)S(1)} %get-tuple-element.132, f32[1,2048]{1,0:T(1,128)S(1)} %get-tuple-element.131, f32[1,2048]{1,0:T(1,128)S(1)} %get-tuple-element.130, f32[1,2048]{1,0:T(1,128)S(1)} %get-tuple-element.129, ...), kind=kLoop, calls=%fused_computation.245 | loop fusion | flops 157696 | bytes 106580 | tf_op jit(solution)/shard_map/add | solution.py:42
  112.6 13.4 %multiply_add_fusion.39 = (f32[1,2048]{1,0:T(1,128)S(1)}, f32[1,2048]{1,0:T(1,128)S(1)}, f32[1,2048]{1,0:T(1,128)S(1)}, f32[1,2048]{1,0:T(1,128)S(1)}, f32[1,204...) fusion(f32[1,2048]{1,0:T(1,128)S(1)} %get-tuple-element.120, ...), kind=kLoop, calls=%fused_computation.274 | loop fusion | flops 174080 | bytes 155732 | tf_op jit(solution)/shard_map/add | solution.py:42
  126.7 13.4 %multiply_add_fusion.11 = f32[1,2048]{1,0:T(1,128)S(1)} fusion(f32[1,2048]{1,0:T(1,128)S(1)} %get-tuple-element.142, f32[1,2048]{1,0:T(1,128)S(1)} %get-tuple-element.141, f32[1,2048]{1,0:T(1,128)S(1)} %get-tuple-element.140, f32[1,2048]{1,0:T(1,128)S(1)} %get-tuple-element.139, f32[1,2048]{1,0:T(1,128)S(1)} %get-tuple-element.138, ...), kind=kLoop, calls=%fused_computation.246 | loop fusion | flops 157696 | bytes 57428 | tf_op jit(solution)/shard_map/add | solution.py:42
  144.8 3.4 collective-permute-start.2
  148.2 6.1 collective-permute-start.3
  154.3 269.9 %while.13 = (s32[]{:T(128)}, f32[21,4096]{0,1:T(8,128)}, f32[4096]{0:T(1024)S(1)}, s32[4,4,4096]{2,1,0:T(4,128)}, f32[21,2048]{0,1:T(8,128)S(1)}, /*index=5*/bf16[4,4,4096]{2,1,0:T(4,128)(2,1)}, s32[]{:T(128)}, s32[]{:T(128)}) while((s32[]{:T(128)}, f32[21,4096]{0,1:T(8,128)}, f32[4096]{0:T(1024)S(1)}, s32[4,4,4096]{2,1,0:T(4,128)}, ...), condition=%wide.region_3.4_spmd.clone, body=%wide.region_0.3_spmd.clone.sunk | while | flops 1335299 | bytes 6324336 | solution.py:113
  155.2 54.4 %gather_fusion = f32[16384,21]{1,0:T(8,128)} fusion(f32[21,2048]{0,1:T(8,128)S(1)} %get-tuple-element.334, s32[16384]{0:T(1024)S(1)} %broadcast_clamp_fusion.2), kind=kCustom, calls=%fused_computation.clone.clone.1 | custom fusion | bytes 2818048 | tf_op jit(solution)/shard_map/while/body/eval_jaxpr/jit(_take)/gather | solution.py:102
  211.2 6.9 multiply_reduce_fusion.2
  221.4 54.4 %gather_fusion = f32[16384,21]{1,0:T(8,128)} fusion(f32[21,2048]{0,1:T(8,128)S(1)} %get-tuple-element.334, s32[16384]{0:T(1024)S(1)} %broadcast_clamp_fusion.2), kind=kCustom, calls=%fused_computation.clone.clone.1 | custom fusion | bytes 2818048 | tf_op jit(solution)/shard_map/while/body/eval_jaxpr/jit(_take)/gather | solution.py:102
  277.5 6.9 multiply_reduce_fusion.2
  284.5 3.1 bitcast_add_fusion.2
  289.3 54.4 %gather_fusion = f32[16384,21]{1,0:T(8,128)} fusion(f32[21,2048]{0,1:T(8,128)S(1)} %get-tuple-element.334, s32[16384]{0:T(1024)S(1)} %broadcast_clamp_fusion.2), kind=kCustom, calls=%fused_computation.clone.clone.1 | custom fusion | bytes 2818048 | tf_op jit(solution)/shard_map/while/body/eval_jaxpr/jit(_take)/gather | solution.py:102
  345.4 6.9 multiply_reduce_fusion.2
  352.3 3.1 bitcast_add_fusion.2
  357.2 54.4 %gather_fusion = f32[16384,21]{1,0:T(8,128)} fusion(f32[21,2048]{0,1:T(8,128)S(1)} %get-tuple-element.334, s32[16384]{0:T(1024)S(1)} %broadcast_clamp_fusion.2), kind=kCustom, calls=%fused_computation.clone.clone.1 | custom fusion | bytes 2818048 | tf_op jit(solution)/shard_map/while/body/eval_jaxpr/jit(_take)/gather | solution.py:102
  413.3 6.9 multiply_reduce_fusion.2
  420.2 3.1 bitcast_add_fusion.2
  427.9 4.6 collective-permute-start.5
  432.5 15.5 %scatter_custom_fusion.1 = f32[4096]{0:T(1024)S(1)} fusion(s32[4096]{0:T(1024)S(1)} %bitcast.174, f32[4096]{0:T(1024)S(1)} %get-tuple-element.37, f32[]{:T(128)} %constant.22.clone.1), kind=kCustom, calls=%fused_computation.299 | custom fusion | bytes 16388 | tf_op jit(solution)/shard_map/scatter | solution.py:189
  449.4 12.0 %scatter_custom_fusion = f32[21,4096]{0,1:T(8,128)} fusion(s32[4096]{0:T(1024)S(1)} %bitcast.175, f32[21,4096]{0,1:T(8,128)S(1)} %copy-done, f32[]{:T(128)} %constant.22.clone.1), kind=kCustom, calls=%fused_computation.13 | custom fusion | bytes 2441220 | tf_op jit(solution)/shard_map/scatter | solution.py:188
  471.2 4.8 collective-permute-done.7
  478.0 3.9 collective-permute-start.9
  483.5 4.3 collective-permute-done.9
  487.9 15.1 %reduce-scatter.3.cloned.1.call-done = f32[21,16,1,8,2,8]{0,5,4,3,2,1:T(8,128)} async-done(((f32[21,16,1,8,2,16]{0,5,4,3,2,1:T(8,128)}), f32[21,16,1,8,2,8]{0,5,4,3,2,1:T(8,128)}) %reduce-scatter.3.cloned.1.call-update) | async-done | bytes 172048 | tf_op jit(solution)/shard_map/reduce_scatter | solution.py:193
  506.1 7.2 %all-to-all-start = ((f32[16,1,2688]{2,1,0:T(1,128)}), f32[16,1,2688]{2,1,0:T(1,128)S(1)}, u32[]{:S(2)}, u32[]{:S(2)}) async-start(f32[16,1,2688]{2,1,0:T(1,128)} %reshape.239), calls=%async_computation.2 | async-start | bytes 344064 | tf_op jit(solution)/shard_map/all_to_all | solution.py:198
  513.3 3.1 collective-permute-start.10
  519.9 4.1 collective-permute-done.11
  528.9 2.8 reshape.241
  531.7 7.5 %all-to-all-start.1 = ((f32[8,1,5376]{2,1,0:T(1,128)}), f32[8,1,5376]{2,1,0:T(1,128)S(1)}, u32[]{:S(2)}, u32[]{:S(2)}) async-start(f32[8,1,5376]{2,1,0:T(1,128)} %reshape.241), calls=%async_computation.3 | async-start | bytes 344064 | tf_op jit(solution)/shard_map/all_to_all | solution.py:197
  540.1 4.5 all-to-all-done.1
  546.6 17.6 %fusion.120 = (f32[1,16,1,8,2,8]{0,5,4,2,1,3:T(8,128)S(1)}, f32[1,16,1,8,2,8]{0,5,4,2,1,3:T(8,128)}, f32[1,16,1,8,2,8]{0,5,4,2,1,3:T(8,128)}, f32[1,16,1,8,2,8]{...) fusion(f32[21,16,1,8,2,8]{0,5,4,2,1,3:T(8,128)S(1)} %bitcast.94), kind=kLoop, calls=%fused_computation.321 | loop fusion | bytes 311296 | tf_op jit(solution)/shard_map/slice | solution.py:165
  565.8 2.7 copy.157
  571.1 2.7 copy.159
  573.8 2.7 copy.160
  579.1 2.7 copy.156
  581.8 2.7 copy.161
  587.1 2.7 copy.163
  592.4 2.7 copy.165
  595.1 2.7 copy.166
  597.7 2.7 copy.167
  603.0 2.7 copy.169
  608.3 2.7 copy.171
  611.0 2.7 copy.172
  613.7 2.7 copy.173
  616.4 2.7 copy.174
  629.3 4.9 collective-permute-start.13
  634.2 3.5 collective-permute-done.12
  639.7 2.8 collective-permute-start.14
  642.4 6.9 collective-permute-start.15
  653.0 4.6 collective-permute-start.17
  657.6 3.4 collective-permute-done.16
  664.9 3.7 collective-permute-start.18
  672.5 4.4 collective-permute-done.19
  677.0 7.9 %collective-permute-start.20 = (f32[3,24,4,8]{1,3,2,0:T(8,128)S(1)}, f32[3,24,4,8]{1,3,2,0:T(8,128)S(1)}, u32[]{:S(2)}, u32[]{:S(2)}) collective-permute-start(f32[3,24,4,8]{1,3,2,0:T(8,128)S(1)} %get-tuple-element.215), channel_id=1, source_target_pairs={{2,0},{4,2},{6,4},{8,6},{10,8},{12,10},{14,12},{3,1},{5,3},{7,5},{... | collective-permute-start | bytes 27656 | tf_op jit(solution)/shard_map/ppermute | solution.py:28
  687.7 6.8 collective-permute-done.21
  694.8 3.6 collective-permute-start.22
  701.0 4.4 collective-permute-done.23
  (230 shorter events, 107.3 us)
Async XLA Ops:
  7.2 8.4 %copy-start.36 = (f32[21]{0:T(128)S(1)}, f32[21]{0:T(128)}, u32[]{:S(2)}) copy-start(f32[21]{0:T(128)} %param.11) | copy-start | bytes 256
  7.2 9.7 %copy-start.38 = (f32[3,2048]{1,0:T(4,128)S(1)}, f32[3,2048]{1,0:T(4,128)}, u32[]{:S(2)}) copy-start(f32[3,2048]{1,0:T(4,128)} %param.10) | copy-start | bytes 73732
  7.2 463.0 %reduce-scatter.5.cloned.1.call-start = ((), (), s32[]{:S(2)}) async-start(), calls=%async_computation.5 | async-start | bytes 196608 | tf_op jit(solution)/shard_map/reduce_scatter | solution.py:194
  8.6 132.2 %copy-start.30 = (s32[16,1,1,4096]{3,2,1,0:T(1,128)S(1)}, s32[16,1,1,4096]{3,2,1,0:T(1,128)}, u32[]{:S(2)}) copy-start(s32[16,1,1,4096]{3,2,1,0:T(1,128)} %param.12) | copy-start | bytes 786436
  8.6 135.2 %collective-permute-start = (f32[6,4,16,8]{1,3,2,0:T(8,128)S(1)}, f32[6,4,16,8]{1,3,2,0:T(8,128)S(1)}, u32[]{:S(2)}, u32[]{:S(2)}) collective-permute-start(f32[6,4,16,8]{1,3,2,0:T(8,128)S(1)} %get-tuple-element.226), channel_id=1, source_target_pairs={{0,16},{16,32},{32,48},{48,64},{64,80},{80,96},{96,112},{112,128},... | collective-permute-start | bytes 36872 | tf_op jit(solution)/shard_map/ppermute | solution.py:26
  10.7 133.2 %collective-permute-start.1 = (f32[6,4,16,8]{1,3,2,0:T(8,128)S(1)}, f32[6,4,16,8]{1,3,2,0:T(8,128)S(1)}, u32[]{:S(2)}, u32[]{:S(2)}) collective-permute-start(f32[6,4,16,8]{1,3,2,0:T(8,128)S(1)} %get-tuple-element.227), channel_id=1, source_target_pairs={{16,0},{32,16},{48,32},{64,48},{80,64},{96,80},{112,96},{128,112},... | collective-permute-start | bytes 36872 | tf_op jit(solution)/shard_map/ppermute | solution.py:28
  143.8 10.4 %copy-start.1 = (f32[6,4,16,8]{1,3,2,0:T(8,128)}, f32[6,4,16,8]{1,3,2,0:T(8,128)S(1)}, u32[]{:S(2)}) copy-start(f32[6,4,16,8]{1,3,2,0:T(8,128)S(1)} %collective-permute-done) | copy-start | bytes 36868
  143.9 10.4 %copy-start.3 = (f32[6,4,16,8]{1,3,2,0:T(8,128)}, f32[6,4,16,8]{1,3,2,0:T(8,128)S(1)}, u32[]{:S(2)}) copy-start(f32[6,4,16,8]{1,3,2,0:T(8,128)S(1)} %collective-permute-done.1) | copy-start | bytes 36868
  144.8 279.4 %collective-permute-start.2 = (f32[6,24,4,8]{1,3,2,0:T(8,128)}, f32[6,24,4,8]{1,3,2,0:T(8,128)}, u32[]{:S(2)}, u32[]{:S(2)}) collective-permute-start(f32[6,24,4,8]{1,3,2,0:T(8,128)} %get-tuple-element.185), channel_id=1, source_target_pairs={{0,2},{2,4},{4,6},{6,8},{8,10},{10,12},{12,14},{1,3},{3,5},{5,7},{... | collective-permute-start | bytes 55304 | tf_op jit(solution)/shard_map/ppermute | solution.py:26
  148.2 276.0 %collective-permute-start.3 = (f32[6,24,4,8]{1,3,2,0:T(8,128)}, f32[6,24,4,8]{1,3,2,0:T(8,128)}, u32[]{:S(2)}, u32[]{:S(2)}) collective-permute-start(f32[6,24,4,8]{1,3,2,0:T(8,128)} %get-tuple-element.186), channel_id=1, source_target_pairs={{2,0},{4,2},{6,4},{8,6},{10,8},{12,10},{14,12},{3,1},{5,3},{7,5},{... | collective-permute-start | bytes 55304 | tf_op jit(solution)/shard_map/ppermute | solution.py:28
  424.2 8.3 %copy-start.40 = (s32[1,1,4096]{2,1,0:T(1,128)S(1)}, s32[1,1,4096]{2,1,0:T(1,128)}, u32[]{:S(2)}) copy-start(s32[1,1,4096]{2,1,0:T(1,128)} %param.14) | copy-start | bytes 49156
  424.2 25.2 %copy-start = (f32[21,4096]{0,1:T(8,128)S(1)}, f32[21,4096]{0,1:T(8,128)}, u32[]{:S(2)}) copy-start(f32[21,4096]{0,1:T(8,128)} %get-tuple-element.36) | copy-start | bytes 1032196
  426.6 35.9 %collective-permute-start.4 = (f32[6,24,24,4]{1,3,2,0:T(4,128)}, f32[6,24,24,4]{1,3,2,0:T(4,128)S(1)}, u32[]{:S(2)}, u32[]{:S(2)}) collective-permute-start(f32[6,24,24,4]{1,3,2,0:T(4,128)} %get-tuple-element.222), channel_id=1, source_target_pairs={{0,1},{2,3},{4,5},{6,7},{8,9},{10,11},{12,13},{14,15},{16,17},{18,... | collective-permute-start | bytes 165896 | tf_op jit(solution)/shard_map/ppermute | solution.py:26
  427.9 34.7 %collective-permute-start.5 = (f32[6,24,24,4]{1,3,2,0:T(4,128)S(1)}, f32[6,24,24,4]{1,3,2,0:T(4,128)S(1)}, u32[]{:S(2)}, u32[]{:S(2)}) collective-permute-start(f32[6,24,24,4]{1,3,2,0:T(4,128)S(1)} %get-tuple-element.223), channel_id=1, source_target_pairs={{1,0},{3,2},{5,4},{7,6},{9,8},{11,10},{13,12},{15,14},{17,16},{19,... | collective-permute-start | bytes 165896 | tf_op jit(solution)/shard_map/ppermute | solution.py:28
  449.1 53.9 %reduce-scatter.3.cloned.1.call-start = ((), (), s32[]{:S(2)}) async-start(), calls=%async_computation.4 | async-start | bytes 3145728 | tf_op jit(solution)/shard_map/reduce_scatter | solution.py:193
  461.4 1.0 copy-start.37
  461.4 1.1 copy-start.2
  461.4 1.3 copy-start.4
  462.4 2.1 copy-start.22
  465.8 5.4 collective-permute-start.6
  467.8 8.2 %collective-permute-start.7 = (f32[3,4,16,8]{1,3,2,0:T(8,128)S(1)}, f32[3,4,16,8]{1,3,2,0:T(8,128)S(1)}, u32[]{:S(2)}, u32[]{:S(2)}) collective-permute-start(f32[3,4,16,8]{1,3,2,0:T(8,128)S(1)} %get-tuple-element.237), channel_id=1, source_target_pairs={{0,16},{16,32},{32,48},{48,64},{64,80},{80,96},{96,112},{112,128},... | collective-permute-start | bytes 18440 | tf_op jit(solution)/shard_map/ppermute | solution.py:26
  476.1 7.4 %collective-permute-start.8 = (f32[3,24,4,8]{1,3,2,0:T(8,128)S(1)}, f32[3,24,4,8]{1,3,2,0:T(8,128)S(1)}, u32[]{:S(2)}, u32[]{:S(2)}) collective-permute-start(f32[3,24,4,8]{1,3,2,0:T(8,128)S(1)} %get-tuple-element.221), channel_id=1, source_target_pairs={{2,0},{4,2},{6,4},{8,6},{10,8},{12,10},{14,12},{3,1},{5,3},{7,5},{... | collective-permute-start | bytes 27656 | tf_op jit(solution)/shard_map/ppermute | solution.py:28
  478.0 9.7 %collective-permute-start.9 = (f32[3,24,4,8]{1,3,2,0:T(8,128)S(1)}, f32[3,24,4,8]{1,3,2,0:T(8,128)S(1)}, u32[]{:S(2)}, u32[]{:S(2)}) collective-permute-start(f32[3,24,4,8]{1,3,2,0:T(8,128)S(1)} %get-tuple-element.220), channel_id=1, source_target_pairs={{0,2},{2,4},{4,6},{6,8},{8,10},{10,12},{12,14},{1,3},{3,5},{5,7},{... | collective-permute-start | bytes 27656 | tf_op jit(solution)/shard_map/ppermute | solution.py:26
  506.1 19.1 %all-to-all-start = ((f32[16,1,2688]{2,1,0:T(1,128)}), f32[16,1,2688]{2,1,0:T(1,128)S(1)}, u32[]{:S(2)}, u32[]{:S(2)}) async-start(f32[16,1,2688]{2,1,0:T(1,128)} %reshape.239), calls=%async_computation.2 | async-start | bytes 344064 | tf_op jit(solution)/shard_map/all_to_all | solution.py:198
  513.3 6.5 collective-permute-start.10
  516.5 7.5 %collective-permute-start.11 = (f32[3,24,24,4]{1,3,2,0:T(4,128)S(1)}, f32[3,24,24,4]{1,3,2,0:T(4,128)S(1)}, u32[]{:S(2)}, u32[]{:S(2)}) collective-permute-start(f32[3,24,24,4]{1,3,2,0:T(4,128)S(1)} %get-tuple-element.231), channel_id=1, source_target_pairs={{0,1},{2,3},{4,5},{6,7},{8,9},{10,11},{12,13},{14,15},{16,17},{18,... | collective-permute-start | bytes 82952 | tf_op jit(solution)/shard_map/ppermute | solution.py:26
  528.9 10.3 %copy-start.5 = (f32[3,24,24,12]{1,3,2,0:T(8,128)S(1)}, f32[3,24,24,12]{1,3,2,0:T(8,128)}, u32[]{:S(2)}) copy-start(f32[3,24,24,12]{1,3,2,0:T(8,128)} %get-tuple-element.211) | copy-start | bytes 248836
  531.7 12.8 %all-to-all-start.1 = ((f32[8,1,5376]{2,1,0:T(1,128)}), f32[8,1,5376]{2,1,0:T(1,128)S(1)}, u32[]{:S(2)}, u32[]{:S(2)}) async-start(f32[8,1,5376]{2,1,0:T(1,128)} %reshape.241), calls=%async_computation.3 | async-start | bytes 344064 | tf_op jit(solution)/shard_map/all_to_all | solution.py:197
  611.0 9.5 %copy-start.6 = (f32[3,16,16,8]{1,3,2,0:T(8,128)S(1)}, f32[3,16,16,8]{1,3,2,0:T(8,128)}, u32[]{:S(2)}) copy-start(f32[3,16,16,8]{1,3,2,0:T(8,128)} %fusion.71) | copy-start | bytes 73732
  620.5 5.3 copy-start.10
  620.5 5.3 copy-start.11
  620.5 5.3 copy-start.15
  620.5 5.3 copy-start.16
  620.5 5.3 copy-start.19
  620.5 5.3 copy-start.28
  620.5 6.0 copy-start.8
  620.5 6.0 copy-start.12
  620.5 6.0 copy-start.13
  620.5 5.9 copy-start.18
  620.6 5.9 copy-start.26
  622.4 4.8 copy-start.7
  622.4 4.8 copy-start.9
  622.4 4.8 copy-start.17
  622.4 4.8 copy-start.24
  627.4 10.3 %collective-permute-start.12 = (f32[6,4,16,8]{1,3,2,0:T(8,128)S(1)}, f32[6,4,16,8]{1,3,2,0:T(8,128)S(1)}, u32[]{:S(2)}, u32[]{:S(2)}) collective-permute-start(f32[6,4,16,8]{1,3,2,0:T(8,128)S(1)} %get-tuple-element.224), channel_id=1, source_target_pairs={{0,16},{16,32},{32,48},{48,64},{64,80},{80,96},{96,112},{112,128},... | collective-permute-start | bytes 36872 | tf_op jit(solution)/shard_map/ppermute | solution.py:26
  629.3 10.1 %collective-permute-start.13 = (f32[6,4,16,8]{1,3,2,0:T(8,128)S(1)}, f32[6,4,16,8]{1,3,2,0:T(8,128)S(1)}, u32[]{:S(2)}, u32[]{:S(2)}) collective-permute-start(f32[6,4,16,8]{1,3,2,0:T(8,128)S(1)} %get-tuple-element.225), channel_id=1, source_target_pairs={{16,0},{32,16},{48,32},{64,48},{80,64},{96,80},{112,96},{128,112},... | collective-permute-start | bytes 36872 | tf_op jit(solution)/shard_map/ppermute | solution.py:28
  639.7 10.1 %collective-permute-start.14 = (f32[6,24,4,8]{1,3,2,0:T(8,128)S(1)}, f32[6,24,4,8]{1,3,2,0:T(8,128)S(1)}, u32[]{:S(2)}, u32[]{:S(2)}) collective-permute-start(f32[6,24,4,8]{1,3,2,0:T(8,128)S(1)} %get-tuple-element.177), channel_id=1, source_target_pairs={{0,2},{2,4},{4,6},{6,8},{8,10},{10,12},{12,14},{1,3},{3,5},{5,7},{... | collective-permute-start | bytes 55304 | tf_op jit(solution)/shard_map/ppermute | solution.py:26
  642.4 8.9 %collective-permute-start.15 = (f32[6,24,4,8]{1,3,2,0:T(8,128)S(1)}, f32[6,24,4,8]{1,3,2,0:T(8,128)S(1)}, u32[]{:S(2)}, u32[]{:S(2)}) collective-permute-start(f32[6,24,4,8]{1,3,2,0:T(8,128)S(1)} %get-tuple-element.178), channel_id=1, source_target_pairs={{2,0},{4,2},{6,4},{8,6},{10,8},{12,10},{14,12},{3,1},{5,3},{7,5},{... | collective-permute-start | bytes 55304 | tf_op jit(solution)/shard_map/ppermute | solution.py:28
  651.7 9.3 %collective-permute-start.16 = (f32[6,24,24,4]{1,3,2,0:T(4,128)S(1)}, f32[6,24,24,4]{1,3,2,0:T(4,128)S(1)}, u32[]{:S(2)}, u32[]{:S(2)}) collective-permute-start(f32[6,24,24,4]{1,3,2,0:T(4,128)S(1)} %get-tuple-element.216), channel_id=1, source_target_pairs={{0,1},{2,3},{4,5},{6,7},{8,9},{10,11},{12,13},{14,15},{16,17},{18,... | collective-permute-start | bytes 165896 | tf_op jit(solution)/shard_map/ppermute | solution.py:26
  653.0 9.2 %collective-permute-start.17 = (f32[6,24,24,4]{1,3,2,0:T(4,128)S(1)}, f32[6,24,24,4]{1,3,2,0:T(4,128)S(1)}, u32[]{:S(2)}, u32[]{:S(2)}) collective-permute-start(f32[6,24,24,4]{1,3,2,0:T(4,128)S(1)} %get-tuple-element.217), channel_id=1, source_target_pairs={{1,0},{3,2},{5,4},{7,6},{9,8},{11,10},{13,12},{15,14},{17,16},{19,... | collective-permute-start | bytes 165896 | tf_op jit(solution)/shard_map/ppermute | solution.py:28
  664.9 7.6 %collective-permute-start.18 = (f32[3,4,16,8]{1,3,2,0:T(8,128)S(1)}, f32[3,4,16,8]{1,3,2,0:T(8,128)S(1)}, u32[]{:S(2)}, u32[]{:S(2)}) collective-permute-start(f32[3,4,16,8]{1,3,2,0:T(8,128)S(1)} %get-tuple-element.233), channel_id=1, source_target_pairs={{16,0},{32,16},{48,32},{64,48},{80,64},{96,80},{112,96},{128,112},... | collective-permute-start | bytes 18440 | tf_op jit(solution)/shard_map/ppermute | solution.py:28
  668.7 8.2 %collective-permute-start.19 = (f32[3,4,16,8]{1,3,2,0:T(8,128)S(1)}, f32[3,4,16,8]{1,3,2,0:T(8,128)S(1)}, u32[]{:S(2)}, u32[]{:S(2)}) collective-permute-start(f32[3,4,16,8]{1,3,2,0:T(8,128)S(1)} %get-tuple-element.232), channel_id=1, source_target_pairs={{0,16},{16,32},{32,48},{48,64},{64,80},{80,96},{96,112},{112,128},... | collective-permute-start | bytes 18440 | tf_op jit(solution)/shard_map/ppermute | solution.py:26
  677.0 10.7 %collective-permute-start.20 = (f32[3,24,4,8]{1,3,2,0:T(8,128)S(1)}, f32[3,24,4,8]{1,3,2,0:T(8,128)S(1)}, u32[]{:S(2)}, u32[]{:S(2)}) collective-permute-start(f32[3,24,4,8]{1,3,2,0:T(8,128)S(1)} %get-tuple-element.215), channel_id=1, source_target_pairs={{2,0},{4,2},{6,4},{8,6},{10,8},{12,10},{14,12},{3,1},{5,3},{7,5},{... | collective-permute-start | bytes 27656 | tf_op jit(solution)/shard_map/ppermute | solution.py:28
  684.9 9.6 %collective-permute-start.21 = (f32[3,24,4,8]{1,3,2,0:T(8,128)S(1)}, f32[3,24,4,8]{1,3,2,0:T(8,128)S(1)}, u32[]{:S(2)}, u32[]{:S(2)}) collective-permute-start(f32[3,24,4,8]{1,3,2,0:T(8,128)S(1)} %get-tuple-element.214), channel_id=1, source_target_pairs={{0,2},{2,4},{4,6},{6,8},{8,10},{10,12},{12,14},{1,3},{3,5},{5,7},{... | collective-permute-start | bytes 27656 | tf_op jit(solution)/shard_map/ppermute | solution.py:26
  694.8 6.3 collective-permute-start.22
  698.4 7.0 collective-permute-start.23
  700.4 5.9 copy-start.20
  700.4 5.9 copy-start.21
  700.5 5.9 copy-start.29
  700.5 5.9 copy-start.35
  700.5 6.0 copy-start.14
  700.5 6.0 copy-start.25
  700.5 6.0 copy-start.34
  705.8 0.9 copy-start.32
  (5 other events, 4.2 us)
Sparse Core Ops, SparseCore 0:
  449.2 13.2 reduce-scatter.4
  465.0 37.8 reduce-scatter.2
where the time goes:
time: 724 us; the launch traced here: 715 us
  local copies, waits for them, and re-layouts  342 us (47%)
  other arithmetic  201 us (28%)
  starting transfers between devices  94.5 us (13%)
  waiting for transfers between devices  62.5 us (9%)
  between operations  15.3 us (2%)
    gather x4, local copies, waits for them, and re-layouts, absorb(): picked = jnp.take(table, chosen, axis=1)  218 us
    add x15, other arithmetic, ordered_sum(): running = running + summand  123 us
    unnamed x114, local copies, waits for them, and re-layouts  67.8 us
    ppermute x12, starting transfers between devices, with_halo(): lax.ppermute(head, axis, [((i + 1) % count, i) for i in range(ends)])  54 us
    ppermute x12, waiting for transfers between devices, with_halo(): lax.ppermute(tail, axis, [(i, (i + 1) % count) for i in range(ends)])  36.1 us
    reduce_sum x4, other arithmetic, absorb(): jnp.sum(picked * masses_wide[None], axis=1)  27.8 us
    ppermute x12, starting transfers between devices, with_halo(): lax.ppermute(tail, axis, [(i, (i + 1) % count) for i in range(ends)])  25.5 us
    slice x2, local copies, waits for them, and re-layouts, advance_stress(): stiffness[symmetric_index(row_index, col_index)] * strain[col_index]  19.2 us
  transfers between devices with their start and end apart: 28, of which 16 were waited for; matrix products, arithmetic and copies ran while one was open for 61% of the time, Pallas kernels for 0%

commit v1 on v0

v1 whole, which is shorter than its diff:
```python
import functools
import math

import jax
import jax.numpy as jnp
from jax import lax
from jax.experimental import pallas as pl
from jax.experimental.pallas import tpu as pltpu
from jax.sharding import PartitionSpec as P

MESH = pl.DeviceIdType.MESH
MERGED = True
STEPS = 2
weights = (0.8, -0.2, 4.0 / 105.0, -1.0 / 280.0)
time_step = 0.2
voigt_pairs = ((0, 0), (1, 1), (2, 2), (1, 2), (0, 2), (0, 1))
upper_pairs = [(row, col) for row in range(6) for col in range(row, 6)]
F32, I32 = jnp.float32, jnp.int32
STRESS_X, STRESS_Y, STRESS_Z = (0, 5, 4), (5, 1, 3), (4, 3, 2)
GX, GY, GA = 16, 8, 2
GRAINS = 16
ROWS = 24
FULL = 32700.0


def upper(first, second):
    return upper_pairs.index((min(first, second), max(first, second)))


def ordered_sum(terms):
    total = terms[0]
    for term in terms[1:]:
        total = total + term
    return total


def lane_pick(row, index):
    return jnp.take_along_axis(row, index, axis=1, mode="promise_in_bounds")


def sublane_pick(block, index):
    return jnp.take_along_axis(block, index, axis=0, mode="promise_in_bounds")


def tree(values, masks):
    for mask in masks:
        values = [
            jnp.where(mask, values[2 * i + 1], values[2 * i]) for i in range(len(values) // 2)
        ]
    return values[0]


def lane_iota(rows):
    return lax.broadcasted_iota(I32, (rows, 128), 1)


def row_iota(rows):
    return lax.broadcasted_iota(I32, (rows, 128), 0)


def rotated_entries(angles, crystal):
    (c1, c0, c2), (s1, s0, s2) = [jnp.cos(a) for a in angles], [jnp.sin(a) for a in angles]
    bunge = [
        [c1 * c2 - s1 * s2 * c0, s1 * c2 + c1 * s2 * c0, s2 * s0],
        [-c1 * s2 - s1 * c2 * c0, -s1 * s2 + c1 * c2 * c0, c2 * s0],
        [s1 * s0, -c1 * s0, c0],
    ]
    rotation = [[bunge[col][row] for col in range(3)] for row in range(3)]
    bond = []
    for i, j in voigt_pairs:
        line = []
        for k, l in voigt_pairs:
            if k == l:
                line.append(rotation[i][k] * rotation[j][k])
            else:
                line.append(rotation[i][k] * rotation[j][l] + rotation[i][l] * rotation[j][k])
        bond.append(line)
    rotated = []
    for row in range(6):
        product = [
            ordered_sum([bond[row][k] * crystal[upper(k, col)] for k in range(6)])
            for col in range(6)
        ]
        for col in range(row, 6):
            rotated.append(ordered_sum([product[k] * bond[col][k] for k in range(6)]))
    return rotated


def prepare(
    euler, crystal, orient, weight, cell_map, angles, entries, table, packed, from_row, from_lane
):
    for j in range(16):
        angles[pl.ds(j, 3, stride=16), :] = euler[:, j * 128 : (j + 1) * 128]
    scalars = [crystal[i] for i in range(21)]
    largest = None
    for half in range(2):
        three = [angles[k * 16 + half * 8 : k * 16 + half * 8 + 8, :] for k in range(3)]
        found = rotated_entries(three, scalars)
        for i, entry in enumerate(found):
            entries[i, half * 8 : half * 8 + 8, :] = entry
            size = jnp.abs(entry)
            largest = size if largest is None else jnp.maximum(largest, size)
    largest = jnp.max(jnp.max(largest, axis=0, keepdims=True), axis=1, keepdims=True)
    largest = jnp.broadcast_to(jnp.maximum(largest, 1e-30), (16, 128))
    scale = FULL / largest
    for pair in range(11):
        high = entries[2 * pair] * scale
        if pair < 10:
            low = jnp.floor(entries[2 * pair + 1] * scale + 0.5)
            high = jnp.floor(high - low * (1.0 / 65536.0) + 0.5).astype(I32)
            table[pair * 16 : pair * 16 + 16, :] = high * 65536 + low.astype(I32)
        else:
            table[pair * 16 : pair * 16 + 16, :] = jnp.floor(high + 0.5).astype(I32) * 65536
    for j in range(32):
        mass = (weight[:, j * 128 : (j + 1) * 128].astype(F32) * 2048.0).astype(I32)
        chosen = orient[pl.ds(j, GRAINS, stride=32), :]
        packed[pl.ds(j, GRAINS, stride=32), :] = chosen * 4096 + mass
    me_x, me_a = lax.axis_index("gx"), lax.axis_index("ga")
    slot = cell_map[...]
    depth = slot & 15
    own = ((depth >> 3) == me_a).astype(I32)
    to_row = own * 16 + (((slot >> 8) - me_x + GX) & 15)
    to_lane = ((slot >> 4) & 15) * 8 + (depth & 7)
    rows, lanes = row_iota(32), row_iota(128)
    here = lane_iota(32).astype(F32)
    found = jnp.zeros((64, 128), F32)
    for j in range(32):
        hit = rows == jnp.broadcast_to(to_row[j : j + 1, :], (32, 128))
        left = jnp.concatenate(
            [jnp.where(hit, float(j), 0.0), jnp.where(hit, here, 0.0)], axis=0
        ).astype(jnp.bfloat16)
        right = jnp.where(lanes == jnp.broadcast_to(to_lane[j : j + 1, :], (128, 128)), 1.0, 0.0)
        found = found + lax.dot_general(
            left,
            right.astype(jnp.bfloat16),
            (((1,), (1,)), ((), ())),
            preferred_element_type=F32,
        )
    found = (found + 0.5).astype(I32)
    from_row[...] = found[:32]
    from_lane[...] = found[32:]
    return largest[:1, :1] * (1.0 / (FULL * 65536.0))


def grain_sums(table, packed, from_row, from_lane, start):
    lane = from_lane[start : start + 8, :]
    row = from_row[start : start + 8, :]
    row_bits = [((row >> bit) & 1) == 1 for bit in range(5)]

    def fetch(grain):
        return tree(
            [
                lane_pick(jnp.broadcast_to(packed[pl.ds(grain * 32 + j, 1), :], (8, 128)), lane)
                for j in range(32)
            ],
            row_bits,
        )

    def absorb(grain, carry):
        word, sums = carry[0], carry[1:]
        following = fetch(jnp.minimum(grain + 1, GRAINS - 1))
        mass = (word & 4095).astype(F32)
        spot = (word >> 12) & 127
        bits = [((word >> (19 + bit)) & 1) == 1 for bit in range(4)]
        out = []
        for pair in range(11):
            value = tree(
                [
                    lane_pick(jnp.broadcast_to(table[pair * 16 + h : pair * 16 + h + 1, :], (8, 128)), spot)
                    for h in range(16)
                ],
                bits,
            )
            out.append(sums[2 * pair] + mass * value.astype(F32))
            if pair < 10:
                out.append(sums[2 * pair + 1] + mass * (value << 16).astype(F32))
        out.append(sums[-1] + mass)
        return (following, *out)

    zero = jnp.zeros((8, 128), F32)
    return lax.fori_loop(0, GRAINS, absorb, (fetch(0),) + (zero,) * 22)[1:]


def block_swap(block, regroup):
    sublane, lane = row_iota(8), lane_iota(8)
    group, place = lane >> 4, lane & 15
    skewed = lane_pick(block, ((group + sublane) & 7) * 16 + place)
    skewed = sublane_pick(skewed, (sublane - group) & 7)
    if regroup:
        y, z = lane & 15, lane >> 4
        group, place = y >> 1, (y & 1) * 8 + z
    return lane_pick(skewed, ((sublane - group) & 7) * 16 + place)


def along_y(field, k, low, high):
    y = lane_iota(16) & 15
    low = pltpu.roll(low, 128 - (4 + 4 * k), 1)
    high = pltpu.roll(high, 16 - 4 * k, 1)
    total = None
    for m in range(1, 5):
        up = pltpu.roll(jnp.where(y < m, high, field), 128 - m, 1)
        down = pltpu.roll(jnp.where(y >= 16 - m, low, field), m, 1)
        term = weights[m - 1] * (up - down)
        total = term if total is None else total + term
    return total


def along_z(field, low, high):
    z = lane_iota(16) >> 4
    total = None
    for m in range(1, 5):
        up = pltpu.roll(jnp.where(z < m, high, field), 128 - 16 * m, 1)
        down = pltpu.roll(jnp.where(z >= 8 - m, low, field), 16 * m, 1)
        term = weights[m - 1] * (up - down)
        total = term if total is None else total + term
    return total


def along_x(padded):
    total = None
    for m in range(1, 5):
        term = weights[m - 1] * (padded[8 + m : 24 + m, :] - padded[8 - m : 24 - m, :])
        total = term if total is None else total + term
    return total


class Halo:
    def __init__(self, step, refs, me):
        self.step, self.me = step, me
        self.xs, self.xl, self.xr, self.xb, self.ys, self.yr, self.zs, self.zr, send, recv = refs
        x, y, a = me
        ends = [((x + 1) % GX, y, a), ((x + GX - 1) % GX, y, a)]
        ends += [(x, (y + 1) % GY, a), (x, (y + GY - 1) % GY, a), (x, y, 1 - a)]
        i = step
        pairs = [
            (self.xs.at[i, :, 8:16], self.xl.at[i]),
            (self.xs.at[i, :, 0:8], self.xr.at[i]),
            (self.ys.at[i, 0], self.yr.at[i, 0]),
            (self.ys.at[i, 1], self.yr.at[i, 1]),
            (self.zs.at[i], self.zr.at[i]),
        ]
        self.copies = [
            pltpu.make_async_remote_copy(
                src_ref=source,
                dst_ref=target,
                send_sem=send.at[i, n],
                recv_sem=recv.at[i, n],
                device_id=end,
                device_id_type=MESH,
            )
            for n, ((source, target), end) in enumerate(zip(pairs, ends))
        ]

    def start(self, along):
        self.fields = along
        fx, fy, fz = along
        i = self.step
        quarter = (lane_iota(16) & 15) >> 2
        for k in range(3):
            self.xs[i, k] = fx[k]
        self.copies[0].start()
        self.copies[1].start()
        for side, offset in ((0, 128 - 12), (1, 0)):
            rolled = [
                pltpu.roll(fy[k], (offset + 4 * k) % 128, 1) if (offset + 4 * k) % 128 else fy[k]
                for k in range(3)
            ]
            self.ys[i, side] = jnp.where(
                quarter == 0, rolled[0], jnp.where(quarter == 1, rolled[1], rolled[2])
            )
            self.copies[2 + side].start()
        for k in range(3):
            self.zs[i, k] = fz[k]
        self.copies[4].start()

    def finish(self):
        x, y, a = self.me
        fx, fy, fz = self.fields
        i = self.step
        for copy in self.copies:
            copy.wait()
        for k in range(3):
            self.xb[k, 0:8, :] = jnp.where(x > 0, self.xl[i, k], 0.0)
            self.xb[k, 8:24, :] = fx[k]
            self.xb[k, 24:32, :] = jnp.where(x < GX - 1, self.xr[i, k], 0.0)
        dx = [along_x(self.xb.at[k]) for k in range(3)]
        low = jnp.where(y > 0, self.yr[i, 0], 0.0)
        high = jnp.where(y < GY - 1, self.yr[i, 1], 0.0)
        dy = [along_y(fy[k], k, low, high) for k in range(3)]
        dz = []
        for k in range(3):
            other = self.zr[i, k]
            dz.append(
                along_z(fz[k], jnp.where(a > 0, other, 0.0), jnp.where(a == 0, other, 0.0))
            )
        return dx, dy, dz


def new_velocity(velocity, diffs, factor):
    dx, dy, dz = diffs
    return [velocity[k] + (dx[k] + dy[k] + dz[k]) * factor for k in range(3)]


def strain_rates(diffs):
    dx, dy, dz = diffs
    return [dx[0], dy[1], dz[2], dy[2] + dz[1], dx[2] + dz[0], dx[1] + dy[0]]


def new_stress(stress, strain, stiffness):
    return [
        stress[row]
        + time_step
        * ordered_sum([stiffness[upper(row, col)] * strain[col] for col in range(6)])
        for row in range(6)
    ]


def stress_parts(stress):
    return tuple([stress[i] for i in which] for which in (STRESS_X, STRESS_Y, STRESS_Z))


def sums_kernel(
    euler, crystal, orient, weight, cell_map, partial, unit, angles, entries, table, packed, row, lane
):
    size = prepare(
        euler, crystal, orient, weight, cell_map, angles, entries, table, packed, row, lane
    )
    unit[...] = jnp.broadcast_to(size, (8, 128))
    for start in (0, 8, 24, 16):
        sums = grain_sums(table, packed, row, lane, start)
        for i in range(22):
            partial[pl.ds(start * ROWS + i, 8, stride=ROWS), :] = sums[i]


def main_kernel(*refs):
    if MERGED:
        euler, crystal, orient, weight, cell_map = refs[:5]
        refs = refs[5:]
    else:
        partial, unit = refs[:2]
        refs = refs[2:]
    density, velocity, stress, stiff_out, velocity_out, stress_out = refs[:6]
    refs = refs[6:]
    if MERGED:
        angles, entries, table, packed, from_row, from_lane, partial = refs[:7]
        refs = refs[7:]
    fields, arrived, first, first_in, second, second_in, stiff = refs[:7]
    rs_send, rs_recv, p1_send, p1_recv, p2_send, p2_recv = refs[7:13]
    halo_refs = refs[13:]

    x, y, a = lax.axis_index("gx"), lax.axis_index("gy"), lax.axis_index("ga")
    barrier = pltpu.get_barrier_semaphore()
    ends = [((x + d) % GX, y, a) for d in range(1, GX)]
    ends += [(x, (y + d) % GY, a) for d in range(1, GY)]
    ends += [(x, y, 1 - a)]
    for end in ends:
        pl.semaphore_signal(barrier, inc=1, device_id=end, device_id_type=MESH)

    for z in range(8):
        lanes = slice(z * 16, z * 16 + 16)
        fields[0:96, lanes] = stress[pl.ds(z, 96, stride=8), :]
        fields[96:144, lanes] = velocity[pl.ds(z, 48, stride=8), :]
        fields[144:160, lanes] = density[pl.ds(z, 16, stride=8), :]
    stresses = [fields[i * 16 : i * 16 + 16, :] for i in range(6)]
    pl.semaphore_wait(barrier, len(ends))

    halos = [Halo(step, halo_refs, (x, y, a)) for step in range(2 * STEPS)]
    halos[0].start(stress_parts(stresses))

    half = [
        pltpu.make_async_remote_copy(
            src_ref=partial.at[pl.ds(i * 8 * ROWS, 8 * ROWS), :],
            dst_ref=arrived.at[pl.ds(i * 8 * ROWS, 8 * ROWS), :],
            send_sem=rs_send.at[i],
            recv_sem=rs_recv.at[i],
            device_id=(x, y, 1 - a),
            device_id_type=MESH,
        )
        for i in range(2)
    ]

    if MERGED:
        size = prepare(
            euler, crystal, orient, weight, cell_map,
            angles, entries, table, packed, from_row, from_lane,
        )
    else:
        half[0].start()
        half[1].start()
        size = unit[:1, :1]

    factor = time_step / fields[144:160, :]
    velocities = [fields[96 + k * 16 : 112 + k * 16, :] for k in range(3)]
    velocities = new_velocity(velocities, halos[0].finish(), factor)
    for k in range(3):
        fields[96 + k * 16 : 112 + k * 16, :] = velocities[k]
    halos[1].start((velocities,) * 3)

    def sums_of(start):
        if MERGED:
            return grain_sums(table, packed, from_row, from_lane, start)
        return [partial[pl.ds(start * ROWS + i, 8, stride=ROWS), :] for i in range(22)]

    if MERGED:
        for i in range(2):
            sums = sums_of(i * 8)
            for c in range(22):
                partial[pl.ds(i * 8 * ROWS + c, 8, stride=ROWS), :] = sums[c]
            half[i].start()
    strain = strain_rates(halos[1].finish())
    for i in range(6):
        fields[144 + i * 16 : 160 + i * 16, :] = strain[i]

    to_brick = [None] * GX
    for d in range(1, GX):
        to_brick[d] = pltpu.make_async_remote_copy(
            src_ref=first.at[pl.ds(d * ROWS, ROWS), :],
            dst_ref=first_in.at[x],
            send_sem=p1_send.at[d - 1],
            recv_sem=p1_recv.at[d - 1],
            device_id=((x + d) % GX, y, a),
            device_id_type=MESH,
        )
    for i in (1, 0):
        sums = sums_of(16 + i * 8)
        half[i].wait()
        base = i * 8 * ROWS
        total = sums[21] + arrived[pl.ds(base + 21, 8, stride=ROWS), :]
        gain = jnp.broadcast_to(size, (8, 128)) / total
        for c in range(21):
            both = sums[c] + arrived[pl.ds(base + c, 8, stride=ROWS), :]
            first[pl.ds(base + c, 8, stride=ROWS), :] = both * gain
        for d in range(i * 8, i * 8 + 8):
            if d:
                to_brick[d].start()
    first_in[x] = first[0:ROWS, :]
    for d in range(1, GX):
        to_brick[d].wait()

    for p in range(2):
        for c in range(21):
            block = first_in[p * 8 : p * 8 + 8, c, :]
            second[pl.ds(p * ROWS + c, 8, stride=2 * ROWS), :] = block_swap(block, False)
    to_y = []
    for d in range(1, GY):
        target = (y + d) % GY
        copy = pltpu.make_async_remote_copy(
            src_ref=second.at[pl.ds(pl.multiple_of(target * 2 * ROWS, 8), 2 * ROWS), :],
            dst_ref=second_in.at[y],
            send_sem=p2_send.at[d - 1],
            recv_sem=p2_recv.at[d - 1],
            device_id=(x, target, a),
            device_id_type=MESH,
        )
        copy.start()
        to_y.append(copy)
    second_in[y] = second[pl.ds(pl.multiple_of(y * 2 * ROWS, 8), 2 * ROWS), :]
    for copy in to_y:
        copy.wait()
    for p in range(2):
        for c in range(21):
            block = second_in[:, p * ROWS + c, :]
            stiff[c, p * 8 : p * 8 + 8, :] = block_swap(block, True)

    strain = [fields[144 + i * 16 : 160 + i * 16, :] for i in range(6)]
    stresses = [fields[i * 16 : i * 16 + 16, :] for i in range(6)]
    stresses = new_stress(stresses, strain, stiff)
    halos[2].start(stress_parts(stresses))
    for r in range(8):
        for p in range(2):
            turned = jnp.transpose(second_in[r, p * ROWS : p * ROWS + ROWS, :], (1, 0))
            for q in range(8):
                row = ((p * 8 + q) * 16 + 2 * r) * 8
                stiff_out[row : row + 16, :] = turned[q * 16 : q * 16 + 16, :21]
    velocities = new_velocity(velocities, halos[2].finish(), factor)
    halos[3].start((velocities,) * 3)
    for k in range(3):
        for z in range(8):
            velocity_out[pl.ds(k * 128 + z, 16, stride=8), :] = velocities[k][:, z * 16 : z * 16 + 16]
    strain = strain_rates(halos[3].finish())
    stresses = new_stress(stresses, strain, stiff)
    for k in range(6):
        for z in range(8):
            stress_out[pl.ds(k * 128 + z, 16, stride=8), :] = stresses[k][:, z * 16 : z * 16 + 16]


def on_device(euler_table, crystal, orient, weight, cell_map, density, velocity, stress):
    vmem, smem = pl.BlockSpec(memory_space=pltpu.VMEM), pl.BlockSpec(memory_space=pltpu.SMEM)
    grains = (
        euler_table,
        crystal,
        orient.reshape(512, 128),
        weight.reshape(GRAINS, 4096),
        cell_map.reshape(32, 128),
    )
    grain_specs = [vmem, smem, vmem, vmem, vmem]
    grain_scratch = [
        pltpu.VMEM((48, 128), F32),
        pltpu.VMEM((21, 16, 128), F32),
        pltpu.VMEM((176, 128), I32),
        pltpu.VMEM((512, 128), I32),
        pltpu.VMEM((32, 128), I32),
        pltpu.VMEM((32, 128), I32),
    ]
    waves = (
        density.transpose(0, 2, 1).reshape(128, 16),
        velocity.transpose(0, 1, 3, 2).reshape(384, 16),
        stress.transpose(0, 1, 3, 2).reshape(768, 16),
    )
    if MERGED:
        operands, specs = grains, grain_specs
        scratch = grain_scratch + [pltpu.VMEM((16 * ROWS, 128), F32)]
    else:
        operands = pl.pallas_call(
            sums_kernel,
            out_shape=(
                jax.ShapeDtypeStruct((32 * ROWS, 128), F32),
                jax.ShapeDtypeStruct((8, 128), F32),
            ),
            in_specs=grain_specs,
            out_specs=(vmem, vmem),
            scratch_shapes=grain_scratch,
            name="grain_sums",
        )(*grains)
        specs, scratch = [vmem, vmem], []
    scratch = scratch + [
        pltpu.VMEM((240, 128), F32),
        pltpu.VMEM((16 * ROWS, 128), F32),
        pltpu.VMEM((16 * ROWS, 128), F32),
        pltpu.VMEM((16, ROWS, 128), F32),
        pltpu.VMEM((16 * ROWS, 128), F32),
        pltpu.VMEM((8, 2 * ROWS, 128), F32),
        pltpu.VMEM((21, 16, 128), F32),
    ]
    for count in (2, 2, 15, 15, 7, 7):
        scratch.append(pltpu.SemaphoreType.DMA((count,)))
    steps = 2 * STEPS
    scratch += [
        pltpu.VMEM((steps, 3, 16, 128), F32),
        pltpu.VMEM((steps, 3, 8, 128), F32),
        pltpu.VMEM((steps, 3, 8, 128), F32),
        pltpu.VMEM((3, 32, 128), F32),
        pltpu.VMEM((steps, 2, 16, 128), F32),
        pltpu.VMEM((steps, 2, 16, 128), F32),
        pltpu.VMEM((steps, 3, 16, 128), F32),
        pltpu.VMEM((steps, 3, 16, 128), F32),
        pltpu.SemaphoreType.DMA((steps, 5)),
        pltpu.SemaphoreType.DMA((steps, 5)),
    ]
    stiffness, velocity, stress = pl.pallas_call(
        main_kernel,
        out_shape=(
            jax.ShapeDtypeStruct((2048, 21), F32),
            jax.ShapeDtypeStruct((384, 16), F32),
            jax.ShapeDtypeStruct((768, 16), F32),
        ),
        in_specs=list(specs) + [vmem, vmem, vmem],
        out_specs=(vmem, vmem, vmem),
        scratch_shapes=scratch,
        compiler_params=pltpu.CompilerParams(
            collective_id=0, has_side_effects=True, vmem_limit_bytes=32 * 1024 * 1024
        ),
        name="relay_and_steps",
    )(*operands, *waves)
    return (
        stiffness.reshape(16, 16, 8, 21).transpose(3, 0, 1, 2),
        velocity.reshape(3, 16, 8, 16).transpose(0, 1, 3, 2),
        stress.reshape(6, 16, 8, 16).transpose(0, 1, 3, 2),
    )


def solution(mesh):
    fields = P(None, "gx", "gy", "ga")
    return jax.shard_map(
        on_device,
        mesh=mesh,
        in_specs=(
            P(),
            P(),
            P("ga", "gx", "gy", None),
            P("ga", "gx", "gy", None),
            P("gx", "gy", None),
            P("gx", "gy", "ga"),
            fields,
            fields,
        ),
        out_specs=(fields, fields, fields),
        check_vma=False,
    )
```

time: 724 us -> 65.7 us (0.09)
  the two profiles are of different devices: /device:TPU:152 before, /device:TPU:32 now
where the time goes in v1:
time: 65.7 us; the launch traced here: 65 us
  Pallas kernels  55.2 us (84%)
  local copies, waits for them, and re-layouts  9.13 us (14%)
  between operations  0.66 us (1%)
    pallas_call x1, Pallas kernels, on_device(): pl.pallas_call(main_kernel, out_shape=(jax.ShapeDtypeStruct((2048, 21), F...  55.2 us
    unnamed x19, local copies, waits for them, and re-layouts  9.13 us

profile of v1, /device:TPU:32, one launch (start us, length us, event | category | flops | bytes accessed | tf_op | source)
XLA Modules:
  0.0 65.0 jit_solution(11801033778716158504)
XLA Ops:
  0.6 0.0 copy-start.7
  0.6 0.6 copy-done.7
  1.3 0.0 copy-start
  1.3 1.0 %copy-done = f32[6,16,16,8]{2,3,1,0:T(8,128)S(1)} copy-done((f32[6,16,16,8]{2,3,1,0:T(8,128)S(1)}, f32[6,16,16,8]{2,3,1,0:T(8,128)}, u32[]{:S(2)}) %copy-start) | copy-done | bytes 49176
  2.3 0.0 copy-start.1
  2.3 0.9 %copy-done.1 = s32[16,1,1,4096]{3,2,1,0:T(1,128)S(1)} copy-done((s32[16,1,1,4096]{3,2,1,0:T(1,128)S(1)}, s32[16,1,1,4096]{3,2,1,0:T(1,128)}, u32[]{:S(2)}) %copy-start.1) | copy-done | bytes 262168
  3.2 0.0 copy-start.2
  3.2 0.9 %copy-done.2 = f32[3,16,16,8]{2,3,1,0:T(8,128)S(1)} copy-done((f32[3,16,16,8]{2,3,1,0:T(8,128)S(1)}, f32[3,16,16,8]{2,3,1,0:T(8,128)}, u32[]{:S(2)}) %copy-start.2) | copy-done | bytes 24600
  4.2 0.0 copy-start.3
  4.2 0.9 %copy-done.3 = bf16[16,1,1,4096]{3,0,2,1:T(8,128)(2,1)S(1)} copy-done((bf16[16,1,1,4096]{3,0,2,1:T(8,128)(2,1)S(1)}, bf16[16,1,1,4096]{3,0,2,1:T(8,128)(2,1)}, u32[]{:S(2)}) %copy-start.3) | copy-done | bytes 131096
  5.1 0.0 copy-start.4
  5.1 0.8 %copy-done.4 = f32[16,16,8]{1,2,0:T(8,128)S(1)} copy-done((f32[16,16,8]{1,2,0:T(8,128)S(1)}, f32[16,16,8]{1,2,0:T(8,128)}, u32[]{:S(2)}) %copy-start.4) | copy-done | bytes 8216
  5.9 0.0 copy-start.5
  5.9 0.8 %copy-done.5 = f32[3,2048]{1,0:T(4,128)S(1)} copy-done((f32[3,2048]{1,0:T(4,128)S(1)}, f32[3,2048]{1,0:T(4,128)}, u32[]{:S(2)}) %copy-start.5) | copy-done | bytes 24600
  6.7 0.0 copy-start.6
  6.7 0.7 %copy-done.6 = s32[1,1,4096]{2,1,0:T(1,128)S(1)} copy-done((s32[1,1,4096]{2,1,0:T(1,128)S(1)}, s32[1,1,4096]{2,1,0:T(1,128)}, u32[]{:S(2)}) %copy-start.6) | copy-done | bytes 16408
  7.4 55.2 %relay_and_steps.1 = (f32[2048,21]{1,0:T(8,128)S(1)}, f32[384,16]{1,0:T(8,128)S(1)}, f32[768,16]{1,0:T(8,128)S(1)}) custom-call(f32[3,2048]{1,0:T(4,128)S(1)} %copy-done.5, f32[21]{0:T(128)S(1)} %copy-done.7, s32[512,128]{1,0:T(8,128)S(1)} %bitcast.24, bf16[16,4096]{1,0:T(8,128)(2,1)S(1)} %bitcast.27, s32[32,128]{1,0:T(8,128)S(1)} %bitcast.29, ...), custom_call_target="tpu_custom_call" | custom-call | tf_op jit(solution)/shard_map/relay_and_steps/pallas_call | solution.py:550
  62.6 1.0 %copy.14 = f32[21,16,16,8]{0,3,2,1:T(8,128)} copy(f32[21,16,16,8]{0,3,2,1:T(8,128)S(1)} %bitcast.21) | data formatting | bytes 344064
  63.6 0.7 %copy.15 = f32[3,16,16,8]{2,3,1,0:T(8,128)} copy(f32[3,16,16,8]{2,3,1,0:T(8,128)S(1)} %bitcast.25) | data formatting | bytes 49152
  64.3 0.7 %copy.16 = f32[6,16,16,8]{2,3,1,0:T(8,128)} copy(f32[6,16,16,8]{2,3,1,0:T(8,128)S(1)} %bitcast.22) | data formatting | bytes 98304
Async XLA Ops:
  0.6 0.7 %copy-start.7 = (f32[21]{0:T(128)S(1)}, f32[21]{0:T(128)}, u32[]{:S(2)}) copy-start(f32[21]{0:T(128)} %refs_1_.1) | copy-start | bytes 256
  1.3 1.0 %copy-start = (f32[6,16,16,8]{2,3,1,0:T(8,128)S(1)}, f32[6,16,16,8]{2,3,1,0:T(8,128)}, u32[]{:S(2)}) copy-start(f32[6,16,16,8]{2,3,1,0:T(8,128)} %param.15) | copy-start | bytes 147460
  2.3 0.9 %copy-start.1 = (s32[16,1,1,4096]{3,2,1,0:T(1,128)S(1)}, s32[16,1,1,4096]{3,2,1,0:T(1,128)}, u32[]{:S(2)}) copy-start(s32[16,1,1,4096]{3,2,1,0:T(1,128)} %param.10) | copy-start | bytes 786436
  3.2 0.9 %copy-start.2 = (f32[3,16,16,8]{2,3,1,0:T(8,128)S(1)}, f32[3,16,16,8]{2,3,1,0:T(8,128)}, u32[]{:S(2)}) copy-start(f32[3,16,16,8]{2,3,1,0:T(8,128)} %param.14) | copy-start | bytes 73732
  4.2 0.9 %copy-start.3 = (bf16[16,1,1,4096]{3,0,2,1:T(8,128)(2,1)S(1)}, bf16[16,1,1,4096]{3,0,2,1:T(8,128)(2,1)}, u32[]{:S(2)}) copy-start(bf16[16,1,1,4096]{3,0,2,1:T(8,128)(2,1)} %param.11) | copy-start | bytes 393220
  5.1 0.8 %copy-start.4 = (f32[16,16,8]{1,2,0:T(8,128)S(1)}, f32[16,16,8]{1,2,0:T(8,128)}, u32[]{:S(2)}) copy-start(f32[16,16,8]{1,2,0:T(8,128)} %param.13) | copy-start | bytes 24580
  5.9 0.8 %copy-start.5 = (f32[3,2048]{1,0:T(4,128)S(1)}, f32[3,2048]{1,0:T(4,128)}, u32[]{:S(2)}) copy-start(f32[3,2048]{1,0:T(4,128)} %refs_0_.1) | copy-start | bytes 73732
  6.7 0.7 %copy-start.6 = (s32[1,1,4096]{2,1,0:T(1,128)S(1)}, s32[1,1,4096]{2,1,0:T(1,128)}, u32[]{:S(2)}) copy-start(s32[1,1,4096]{2,1,0:T(1,128)} %param.12) | copy-start | bytes 49156

commit v2 on v1

v2 whole, which is shorter than its diff:
```python
import jax
import jax.numpy as jnp
import numpy as np
from jax import lax
from jax.experimental import pallas as pl
from jax.experimental.pallas import tpu as pltpu
from jax.sharding import PartitionSpec as P

MESH = pl.DeviceIdType.MESH
STEPS = 2
weights = (0.8, -0.2, 4.0 / 105.0, -1.0 / 280.0)
time_step = 0.2
voigt_pairs = ((0, 0), (1, 1), (2, 2), (1, 2), (0, 2), (0, 1))
upper_pairs = [(row, col) for row in range(6) for col in range(row, 6)]
F32, I32 = jnp.float32, jnp.int32
STRESS_X, STRESS_Y, STRESS_Z = (0, 5, 4), (5, 1, 3), (4, 3, 2)
GX, GY, GA = 16, 8, 2
GRAINS = 16
PARTS = 19
ROWS = 24
FULL = 32767.0
NEAR = 4


def upper(first, second):
    return upper_pairs.index((min(first, second), max(first, second)))


def ordered_sum(terms):
    total = terms[0]
    for term in terms[1:]:
        total = total + term
    return total


def entry_map(rotation):
    bond = np.zeros((6, 6))
    for i, (p, q) in enumerate(voigt_pairs):
        for j, (k, l) in enumerate(voigt_pairs):
            bond[i, j] = rotation[p, k] * rotation[q, l]
            if k != l:
                bond[i, j] += rotation[p, l] * rotation[q, k]
    image = np.zeros((21, 21))
    for n, (row, col) in enumerate(upper_pairs):
        unit = np.zeros((6, 6))
        unit[row, col] = unit[col, row] = 1.0
        turned = bond @ unit @ bond.T
        image[:, n] = [turned[i, j] for i, j in upper_pairs]
    return image


def turn(axis, angle):
    i, j = (axis + 1) % 3, (axis + 2) % 3
    out = np.eye(3)
    out[i, i] = out[j, j] = np.cos(angle)
    out[j, i] = np.sin(angle)
    out[i, j] = -out[j, i]
    return out


def harmonic_parts():
    size = np.sqrt([(1.0 + (r > 2)) * (1 + (c > 2)) * (1 + (r != c)) for r, c in upper_pairs])
    spins = []
    for axis in range(3):
        spin = np.zeros((21, 21))
        for n in range(16):
            angle = 2 * np.pi * n / 16
            image = size[:, None] * entry_map(turn(axis, angle)) / size
            spin += sum(m * np.sin(m * angle) for m in range(1, 5)) / 8 * image
        spins.append(spin)
    unit = np.eye(21)
    square = -(spins[0] @ spins[0] + spins[1] @ spins[1] + spins[2] @ spins[2])
    level = spins[2] @ spins[2]
    flat = unit
    for m in range(1, 5):
        flat = flat @ (unit + level / m**2)
    chosen = {0: (0, 1), 2: (upper(2, 2), upper(0, 1)), 4: (upper(2, 2),)}
    parts = []
    for degree, seeds in chosen.items():
        keep = flat
        for other in (0, 2, 4):
            if other != degree:
                first, last = degree * (degree + 1), other * (other + 1)
                keep = keep @ (square - last * unit) / (first - last)
        heads = []
        for seed in seeds:
            head = keep[:, seed]
            for former in heads:
                head = head - former * (former @ head)
            heads.append(head / np.linalg.norm(head))
            chain = [heads[-1]]
            for m in range(degree):
                step = spins[1] @ chain[m]
                if m:
                    step = step - chain[m - 1] * (chain[m - 1] @ step)
                chain.append(step / np.linalg.norm(step))
            part = [chain[0]]
            for m in range(1, degree + 1):
                part += [chain[m], spins[2] @ chain[m] / m]
            parts.append(np.stack(part, axis=1))
    basis = np.concatenate(parts[2:], axis=1)
    even = np.concatenate(parts[:2], axis=1)
    quarter = basis.T @ (size[:, None] * entry_map(turn(1, np.pi / 2)) / size) @ basis
    tables = (basis.T * size, basis / size[:, None], (even @ even.T) / size[:, None] * size, quarter)
    return [np.round(table, 9) for table in tables]


TO_PARTS, FROM_PARTS, EVEN, QUARTER = harmonic_parts()
BLOCKS = ((0, 2), (5, 2), (10, 4))


def sparse(row, values):
    terms = []
    for k in range(len(values)):
        factor = float(row[k])
        if factor:
            terms.append(values[k] if factor == 1 else -values[k] if factor == -1 else factor * values[k])
    return ordered_sum(terms) if terms else None


def quarter_turn(parts, matrix):
    out = []
    for start, degree in BLOCKS:
        stop = start + 2 * degree + 1
        out += [sparse(matrix[i, start:stop], parts[start:stop]) for i in range(start, stop)]
    return out


def about_z(parts, cos, sin):
    out = []
    for start, degree in BLOCKS:
        out.append(parts[start] if cos[0] is None else parts[start] * cos[0])
        for m in range(1, degree + 1):
            a, b = parts[start + 2 * m - 1], parts[start + 2 * m]
            out += [a * cos[m] - b * sin[m], a * sin[m] + b * cos[m]]
    return out


def multiples(cos, sin):
    twice = cos + cos
    cos, sin = [None, cos, twice * cos - 1.0], [None, sin, twice * sin]
    for m in (3, 4):
        cos.append(twice * cos[m - 1] - cos[m - 2])
        sin.append(twice * sin[m - 1] - sin[m - 2])
    return cos, sin


def lane_pick(row, index):
    return jnp.take_along_axis(row, index, axis=1, mode="promise_in_bounds")


def sublane_pick(block, index):
    return jnp.take_along_axis(block, index, axis=0, mode="promise_in_bounds")


def tree(values, masks):
    for mask in masks:
        values = [
            jnp.where(mask, values[2 * i + 1], values[2 * i]) for i in range(len(values) // 2)
        ]
    return values[0]


def lane_iota(rows):
    return lax.broadcasted_iota(I32, (rows, 128), 1)


def row_iota(rows):
    return lax.broadcasted_iota(I32, (rows, 128), 0)


def pair_word(first, second):
    low = jnp.floor(second * FULL + 0.5)
    high = jnp.floor(first * FULL - low * (1.0 / 65536.0) + 0.5).astype(I32)
    return high * 65536 + low.astype(I32)


def prepare_table(euler, crystal, angles, table, seeds, even):
    for j in range(16):
        angles[pl.ds(j, 3, stride=16), :] = euler[:, j * 128 : (j + 1) * 128]
    for k in range(3):
        angle = angles[k * 16 : k * 16 + 16, :]
        table[k * 16 : k * 16 + 16, :] = pair_word(jnp.cos(angle), jnp.sin(angle))
    values = [jnp.full((8, 128), crystal[i], F32) for i in range(21)]
    for i in range(PARTS):
        seeds[i] = sparse(TO_PARTS[i], values)
    for i in range(21):
        found = sparse(EVEN[i], values)
        even[i] = jnp.zeros((8, 128), F32) if found is None else found


def prepare_cells(orient, weight, cell_map, packed, from_row, from_lane):
    for j in range(32):
        mass = (weight[:, j * 128 : (j + 1) * 128].astype(F32) * 2048.0).astype(I32)
        chosen = orient[pl.ds(j, GRAINS, stride=32), :]
        packed[pl.ds(j, GRAINS, stride=32), :] = chosen * 4096 + mass
    me_x, me_a = lax.axis_index("gx"), lax.axis_index("ga")
    slot = cell_map[...]
    depth = slot & 15
    own = ((depth >> 3) == me_a).astype(I32)
    to_row = own * 16 + (((slot >> 8) - me_x + (GX - NEAR)) & 15)
    to_lane = ((slot >> 4) & 15) * 8 + (depth & 7)
    rows, lanes = row_iota(32), row_iota(128)
    here = lane_iota(32).astype(F32)
    found = jnp.zeros((64, 128), F32)
    for j in range(32):
        hit = rows == jnp.broadcast_to(to_row[j : j + 1, :], (32, 128))
        left = jnp.concatenate(
            [jnp.where(hit, float(j), 0.0), jnp.where(hit, here, 0.0)], axis=0
        ).astype(jnp.bfloat16)
        right = jnp.where(lanes == jnp.broadcast_to(to_lane[j : j + 1, :], (128, 128)), 1.0, 0.0)
        found = found + lax.dot_general(
            left,
            right.astype(jnp.bfloat16),
            (((1,), (1,)), ((), ())),
            preferred_element_type=F32,
        )
    found = (found + 0.5).astype(I32)
    from_row[...] = found[:32]
    from_lane[...] = found[32:]


def grain_sums(table, seeds, packed, from_row, from_lane, start):
    lane = from_lane[start : start + 8, :]
    row = from_row[start : start + 8, :]
    row_bits = [((row >> bit) & 1) == 1 for bit in range(5)]

    def fetch(grain):
        return tree(
            [
                lane_pick(jnp.broadcast_to(packed[pl.ds(grain * 32 + j, 1), :], (8, 128)), lane)
                for j in range(32)
            ],
            row_bits,
        )

    def angles_of(word):
        spot = (word >> 12) & 127
        bits = [((word >> (19 + bit)) & 1) == 1 for bit in range(4)]
        return [
            tree(
                [
                    lane_pick(
                        jnp.broadcast_to(table[k * 16 + h : k * 16 + h + 1, :], (8, 128)), spot
                    )
                    for h in range(16)
                ],
                bits,
            )
            for k in range(3)
        ]

    def absorb(grain, carry):
        word, pairs, sums = carry[0], carry[1:4], carry[4:]
        coming = carry[0 + 4 + PARTS + 1]
        sums = sums[: PARTS + 1]
        after = fetch(jnp.minimum(grain + 2, GRAINS - 1))
        coming_pairs = angles_of(coming)
        mass = (word & 4095).astype(F32)
        unit = 1.0 / (FULL * 65536.0)
        turns = [
            multiples(pair.astype(F32) * unit, (pair << 16).astype(F32) * unit) for pair in pairs
        ]
        cos, sin = turns[2]
        cos = [mass] + [mass * value for value in cos[1:]]
        sin = [None] + [mass * value for value in sin[1:]]
        parts = about_z([seeds[i] for i in range(PARTS)], cos, sin)
        parts = quarter_turn(parts, QUARTER.T)
        parts = about_z(parts, *turns[1])
        parts = quarter_turn(parts, QUARTER)
        parts = about_z(parts, *turns[0])
        out = [old + new for old, new in zip(sums, parts)] + [sums[PARTS] + mass]
        return (coming, *coming_pairs, *out, after)

    zero = jnp.zeros((8, 128), F32)
    first, second = fetch(0), fetch(1)
    carry = (first, *angles_of(first)) + (zero,) * (PARTS + 1) + (second,)
    return lax.fori_loop(0, GRAINS, absorb, carry)[4 : 4 + PARTS + 1]


def block_swap(block, regroup):
    sublane, lane = row_iota(8), lane_iota(8)
    group, place = lane >> 4, lane & 15
    skewed = lane_pick(block, ((group + sublane) & 7) * 16 + place)
    skewed = sublane_pick(skewed, (sublane - group) & 7)
    if regroup:
        y, z = lane & 15, lane >> 4
        group, place = y >> 1, (y & 1) * 8 + z
    return lane_pick(skewed, ((sublane - group) & 7) * 16 + place)


def along_y(field, k, low, high):
    y = lane_iota(16) & 15
    low = pltpu.roll(low, 128 - (4 + 4 * k), 1)
    high = pltpu.roll(high, 16 - 4 * k, 1)
    total = None
    for m in range(1, 5):
        up = pltpu.roll(jnp.where(y < m, high, field), 128 - m, 1)
        down = pltpu.roll(jnp.where(y >= 16 - m, low, field), m, 1)
        term = weights[m - 1] * (up - down)
        total = term if total is None else total + term
    return total


def along_z(field, low, high):
    z = lane_iota(16) >> 4
    total = None
    for m in range(1, 5):
        up = pltpu.roll(jnp.where(z < m, high, field), 128 - 16 * m, 1)
        down = pltpu.roll(jnp.where(z >= 8 - m, low, field), 16 * m, 1)
        term = weights[m - 1] * (up - down)
        total = term if total is None else total + term
    return total


def along_x(padded):
    total = None
    for m in range(1, 5):
        term = weights[m - 1] * (padded[8 + m : 24 + m, :] - padded[8 - m : 24 - m, :])
        total = term if total is None else total + term
    return total


class Halo:
    def __init__(self, step, refs, me):
        self.step, self.me = step, me
        self.xs, self.xl, self.xr, self.xb, self.ys, self.yr, self.zs, self.zr, send, recv = refs
        x, y, a = me
        ends = [((x + 1) % GX, y, a), ((x + GX - 1) % GX, y, a)]
        ends += [(x, (y + 1) % GY, a), (x, (y + GY - 1) % GY, a), (x, y, 1 - a)]
        i = step
        pairs = [
            (self.xs.at[i, :, 8:16], self.xl.at[i]),
            (self.xs.at[i, :, 0:8], self.xr.at[i]),
            (self.ys.at[i, 0], self.yr.at[i, 0]),
            (self.ys.at[i, 1], self.yr.at[i, 1]),
            (self.zs.at[i], self.zr.at[i]),
        ]
        self.copies = [
            pltpu.make_async_remote_copy(
                src_ref=source,
                dst_ref=target,
                send_sem=send.at[i, n],
                recv_sem=recv.at[i, n],
                device_id=end,
                device_id_type=MESH,
            )
            for n, ((source, target), end) in enumerate(zip(pairs, ends))
        ]

    def start(self, along):
        self.fields = along
        fx, fy, fz = along
        i = self.step
        quarter = (lane_iota(16) & 15) >> 2
        for k in range(3):
            self.xs[i, k] = fx[k]
        self.copies[0].start()
        self.copies[1].start()
        for side, offset in ((0, 128 - 12), (1, 0)):
            rolled = [
                pltpu.roll(fy[k], (offset + 4 * k) % 128, 1) if (offset + 4 * k) % 128 else fy[k]
                for k in range(3)
            ]
            self.ys[i, side] = jnp.where(
                quarter == 0, rolled[0], jnp.where(quarter == 1, rolled[1], rolled[2])
            )
            self.copies[2 + side].start()
        for k in range(3):
            self.zs[i, k] = fz[k]
        self.copies[4].start()

    def finish(self):
        x, y, a = self.me
        fx, fy, fz = self.fields
        i = self.step
        for copy in self.copies:
            copy.wait()
        for k in range(3):
            self.xb[k, 0:8, :] = jnp.where(x > 0, self.xl[i, k], 0.0)
            self.xb[k, 8:24, :] = fx[k]
            self.xb[k, 24:32, :] = jnp.where(x < GX - 1, self.xr[i, k], 0.0)
        dx = [along_x(self.xb.at[k]) for k in range(3)]
        low = jnp.where(y > 0, self.yr[i, 0], 0.0)
        high = jnp.where(y < GY - 1, self.yr[i, 1], 0.0)
        dy = [along_y(fy[k], k, low, high) for k in range(3)]
        dz = []
        for k in range(3):
            other = self.zr[i, k]
            dz.append(
                along_z(fz[k], jnp.where(a > 0, other, 0.0), jnp.where(a == 0, other, 0.0))
            )
        return dx, dy, dz


def new_velocity(velocity, diffs, factor):
    dx, dy, dz = diffs
    return [velocity[k] + (dx[k] + dy[k] + dz[k]) * factor for k in range(3)]


def strain_rates(diffs):
    dx, dy, dz = diffs
    return [dx[0], dy[1], dz[2], dy[2] + dz[1], dx[2] + dz[0], dx[1] + dy[0]]


def new_stress(stress, strain, stiffness):
    return [
        stress[row]
        + time_step
        * ordered_sum([stiffness[upper(row, col)] * strain[col] for col in range(6)])
        for row in range(6)
    ]


def stress_parts(stress):
    return tuple([stress[i] for i in which] for which in (STRESS_X, STRESS_Y, STRESS_Z))


def entries_of(parts, even):
    out = []
    for i in range(21):
        entry = sparse(FROM_PARTS[i], parts)
        if EVEN[i].any():
            constant = jnp.concatenate([even[i], even[i]], axis=0)
            entry = constant if entry is None else entry + constant
        out.append(entry)
    return out


def main_kernel(*refs):
    given, outs, refs = refs[:8], refs[8:11], refs[11:]
    stiff_out, velocity_out, stress_out = outs
    held, refs = refs[:8], refs[8:]
    angles, table, seeds, even, packed, from_row, from_lane, partial = refs[:8]
    refs = refs[8:]
    fields, arrived, first, first_in, second, second_in, stiff, load_sem = refs[:8]
    rs_send, rs_recv, p1_send, p1_recv, p2_send, p2_recv = refs[8:14]
    halo_refs = refs[14:]

    loads = [pltpu.make_async_copy(given[i], held[i], load_sem.at[i]) for i in range(8)]
    for load in loads:
        load.start()
    euler, crystal, orient, weight, cell_map, density, velocity, stress = held
    x, y, a = lax.axis_index("gx"), lax.axis_index("gy"), lax.axis_index("ga")
    barrier = pltpu.get_barrier_semaphore()
    ends = [((x + d) % GX, y, a) for d in range(1, GX)]
    ends += [(x, (y + d) % GY, a) for d in range(1, GY)]
    ends += [(x, y, 1 - a)]
    for end in ends:
        pl.semaphore_signal(barrier, inc=1, device_id=end, device_id_type=MESH)

    for i in range(5):
        loads[i].wait()
    prepare_table(euler, crystal, angles, table, seeds, even)
    prepare_cells(orient, weight, cell_map, packed, from_row, from_lane)

    halos = [Halo(step, halo_refs, (x, y, a)) for step in range(2 * STEPS)]
    half = [
        pltpu.make_async_remote_copy(
            src_ref=partial.at[pl.ds(i * 8, 8), 0 : PARTS + 1],
            dst_ref=arrived.at[pl.ds(i * 8, 8), 0 : PARTS + 1],
            send_sem=rs_send.at[i],
            recv_sem=rs_recv.at[i],
            device_id=(x, y, 1 - a),
            device_id_type=MESH,
        )
        for i in range(2)
    ]
    to_brick = {}
    for row in range(16):
        d = (row + NEAR) % GX
        if d:
            to_brick[row] = pltpu.make_async_remote_copy(
                src_ref=first.at[row, 0:PARTS],
                dst_ref=first_in.at[x, 0:PARTS],
                send_sem=p1_send.at[d - 1],
                recv_sem=p1_recv.at[d - 1],
                device_id=((x + d) % GX, y, a),
                device_id_type=MESH,
            )

    def sums_of(start):
        return grain_sums(table, seeds, packed, from_row, from_lane, start)

    def other_half(i):
        sums = sums_of(i * 8)
        for c in range(PARTS + 1):
            partial[i * 8 : i * 8 + 8, c, :] = sums[c]

    def own_half(i):
        sums = sums_of(16 + i * 8)
        half[i].wait()
        rows = slice(i * 8, i * 8 + 8)
        gain = 1.0 / (sums[PARTS] + arrived[rows, PARTS, :])
        for c in range(PARTS):
            first[rows, c, :] = (sums[c] + arrived[rows, c, :]) * gain
        for row in range(i * 8, i * 8 + 8):
            if row in to_brick:
                to_brick[row].start()

    other_half(0)
    for i in range(5, 8):
        loads[i].wait()
    for z in range(8):
        lanes = slice(z * 16, z * 16 + 16)
        fields[0:96, lanes] = stress[pl.ds(z, 96, stride=8), :]
        fields[96:144, lanes] = velocity[pl.ds(z, 48, stride=8), :]
        fields[144:160, lanes] = density[pl.ds(z, 16, stride=8), :]
    stresses = [fields[i * 16 : i * 16 + 16, :] for i in range(6)]
    pl.semaphore_wait(barrier, len(ends))
    half[0].start()
    halos[0].start(stress_parts(stresses))
    other_half(1)
    half[1].start()
    own_half(0)
    factor = time_step / fields[144:160, :]
    velocities = [fields[96 + k * 16 : 112 + k * 16, :] for k in range(3)]
    velocities = new_velocity(velocities, halos[0].finish(), factor)
    for k in range(3):
        fields[96 + k * 16 : 112 + k * 16, :] = velocities[k]
    fields[144:160, :] = factor
    halos[1].start((velocities,) * 3)
    own_half(1)
    velocities = [fields[96 + k * 16 : 112 + k * 16, :] for k in range(3)]
    halos[1].fields = (velocities,) * 3
    strain = strain_rates(halos[1].finish())
    for i in range(6):
        fields[160 + i * 16 : 176 + i * 16, :] = strain[i]
    first_in[x, 0:PARTS, :] = first[GX - NEAR, 0:PARTS, :]
    for copy in to_brick.values():
        copy.wait()

    for p in range(2):
        for c in range(PARTS):
            block = first_in[p * 8 : p * 8 + 8, c, :]
            second[:, p, c, :] = block_swap(block, False)
    to_y = []
    for d in range(1, GY):
        target = (y + d) % GY
        copy = pltpu.make_async_remote_copy(
            src_ref=second.at[target, :, 0:PARTS],
            dst_ref=second_in.at[y, :, 0:PARTS],
            send_sem=p2_send.at[d - 1],
            recv_sem=p2_recv.at[d - 1],
            device_id=(x, target, a),
            device_id_type=MESH,
        )
        copy.start()
        to_y.append(copy)
    for p in range(2):
        second_in[y, p, 0:PARTS, :] = second[y, p, 0:PARTS, :]
    for copy in to_y:
        copy.wait()
    parts = []
    for c in range(PARTS):
        parts.append(
            jnp.concatenate([block_swap(second_in[:, p, c, :], True) for p in range(2)], axis=0)
        )
    for i, entry in enumerate(entries_of(parts, even)):
        stiff[i] = entry

    strain = [fields[160 + i * 16 : 176 + i * 16, :] for i in range(6)]
    stresses = [fields[i * 16 : i * 16 + 16, :] for i in range(6)]
    stresses = new_stress(stresses, strain, stiff)
    halos[2].start(stress_parts(stresses))
    for row in range(16):
        turned = jnp.transpose(stiff[:, row, :], (1, 0))
        for z in range(8):
            stiff_out[pl.ds(row * 128 + z, 16, stride=8), :] = turned[z * 16 : z * 16 + 16, :21]
    factor = fields[144:160, :]
    velocities = [fields[96 + k * 16 : 112 + k * 16, :] for k in range(3)]
    velocities = new_velocity(velocities, halos[2].finish(), factor)
    halos[3].start((velocities,) * 3)
    for k in range(3):
        for z in range(8):
            velocity_out[pl.ds(k * 128 + z, 16, stride=8), :] = velocities[k][:, z * 16 : z * 16 + 16]
    strain = strain_rates(halos[3].finish())
    stresses = new_stress(stresses, strain, stiff)
    for k in range(6):
        for z in range(8):
            stress_out[pl.ds(k * 128 + z, 16, stride=8), :] = stresses[k][:, z * 16 : z * 16 + 16]


def on_device(euler_table, crystal, orient, weight, cell_map, density, velocity, stress):
    anywhere, vmem = pl.BlockSpec(memory_space=pl.ANY), pl.BlockSpec(memory_space=pltpu.VMEM)
    operands = (
        euler_table,
        crystal,
        orient.reshape(512, 128),
        weight.reshape(GRAINS, 4096),
        cell_map.reshape(32, 128),
        density.transpose(0, 2, 1).reshape(128, 16),
        velocity.transpose(0, 1, 3, 2).reshape(384, 16),
        stress.transpose(0, 1, 3, 2).reshape(768, 16),
    )
    scratch = [
        (pltpu.SMEM if i == 1 else pltpu.VMEM)(array.shape, array.dtype)
        for i, array in enumerate(operands)
    ]
    scratch += [
        pltpu.VMEM((48, 128), F32),
        pltpu.VMEM((48, 128), I32),
        pltpu.VMEM((PARTS, 8, 128), F32),
        pltpu.VMEM((21, 8, 128), F32),
        pltpu.VMEM((512, 128), I32),
        pltpu.VMEM((32, 128), I32),
        pltpu.VMEM((32, 128), I32),
        pltpu.VMEM((16, ROWS, 128), F32),
        pltpu.VMEM((256, 128), F32),
        pltpu.VMEM((16, ROWS, 128), F32),
        pltpu.VMEM((16, ROWS, 128), F32),
        pltpu.VMEM((16, ROWS, 128), F32),
        pltpu.VMEM((8, 2, ROWS, 128), F32),
        pltpu.VMEM((8, 2, ROWS, 128), F32),
        pltpu.VMEM((21, 16, 128), F32),
    ]
    for count in (8, 2, 2, 15, 15, 7, 7):
        scratch.append(pltpu.SemaphoreType.DMA((count,)))
    steps = 2 * STEPS
    scratch += [
        pltpu.VMEM((steps, 3, 16, 128), F32),
        pltpu.VMEM((steps, 3, 8, 128), F32),
        pltpu.VMEM((steps, 3, 8, 128), F32),
        pltpu.VMEM((3, 32, 128), F32),
        pltpu.VMEM((steps, 2, 16, 128), F32),
        pltpu.VMEM((steps, 2, 16, 128), F32),
        pltpu.VMEM((steps, 3, 16, 128), F32),
        pltpu.VMEM((steps, 3, 16, 128), F32),
        pltpu.SemaphoreType.DMA((steps, 5)),
        pltpu.SemaphoreType.DMA((steps, 5)),
    ]
    stiffness, velocity, stress = pl.pallas_call(
        main_kernel,
        out_shape=(
            jax.ShapeDtypeStruct((2048, 21), F32),
            jax.ShapeDtypeStruct((384, 16), F32),
            jax.ShapeDtypeStruct((768, 16), F32),
        ),
        in_specs=[anywhere] * 8,
        out_specs=(vmem, vmem, vmem),
        scratch_shapes=scratch,
        compiler_params=pltpu.CompilerParams(
            collective_id=0, has_side_effects=True, vmem_limit_bytes=56 * 1024 * 1024
        ),
        name="relay_and_steps",
    )(*operands)
    return (
        stiffness.reshape(16, 16, 8, 21).transpose(3, 0, 1, 2),
        velocity.reshape(3, 16, 8, 16).transpose(0, 1, 3, 2),
        stress.reshape(6, 16, 8, 16).transpose(0, 1, 3, 2),
    )


def solution(mesh):
    fields = P(None, "gx", "gy", "ga")
    return jax.shard_map(
        on_device,
        mesh=mesh,
        in_specs=(
            P(),
            P(),
            P("ga", "gx", "gy", None),
            P("ga", "gx", "gy", None),
            P("gx", "gy", None),
            P("gx", "gy", "ga"),
            fields,
            fields,
        ),
        out_specs=(fields, fields, fields),
        check_vma=False,
    )
```

time: 65.7 us -> 45.8 us (0.70)
  Pallas kernels: 55.2 us -> 40.6 us
  local copies, waits for them, and re-layouts: 9.13 us -> 4.15 us
    pallas_call x1, Pallas kernels: 55.2 us -> 40.6 us  [on_device(): pl.pallas_call(main_kernel, out_shape=(jax.ShapeDtypeStruct((2048, 21), F...]
    unnamed x19 -> x7, local copies, waits for them, and re-layouts: 9.13 us -> 4.15 us
where the time goes in v2:
time: 45.8 us; the launch traced here: 45.4 us
  Pallas kernels  40.6 us (89%)
  local copies, waits for them, and re-layouts  4.15 us (9%)
  between operations  0.65 us (1%)
    pallas_call x1, Pallas kernels, on_device(): pl.pallas_call(main_kernel, out_shape=(jax.ShapeDtypeStruct((2048, 21), F...  40.6 us
    unnamed x7, local copies, waits for them, and re-layouts  4.15 us

profile of v2, /device:TPU:32, one launch (start us, length us, event | category | flops | bytes accessed | tf_op | source)
XLA Modules:
  0.0 45.4 jit_solution(17920555914361971690)
XLA Ops:
  0.6 40.6 %relay_and_steps.1 = (f32[2048,21]{1,0:T(8,128)}, f32[384,16]{1,0:T(8,128)}, f32[768,16]{1,0:T(8,128)}) custom-call(f32[3,2048]{1,0:T(4,128)} %refs_0_.1, f32[21]{0:T(128)} %refs_1_.1, s32[512,128]{1,0:T(8,128)} %bitcast.24, bf16[16,4096]{1,0:T(8,128)(2,1)} %bitcast.27, s32[32,128]{1,0:T(8,128)} %bitcast.29, f32[128,16]{1,0:T(8,128)} %bitcast.28, ...), custom_call_target="tpu_custom_call" | custom-call | tf_op jit(solution)/shard_map/relay_and_steps/pallas_call | solution.py:632
  41.3 0.0 copy-start.1
  41.3 2.3 %copy.14 = f32[21,16,16,8]{0,3,2,1:T(8,128)} copy(f32[21,16,16,8]{0,3,2,1:T(8,128)} %bitcast.21) | data formatting | bytes 344064
  43.6 0.0 copy-done.1
  43.6 0.0 copy-start
  43.6 0.7 %copy.15 = f32[3,16,16,8]{2,3,1,0:T(8,128)} copy(f32[3,16,16,8]{2,3,1,0:T(8,128)S(1)} %bitcast.25) | data formatting | bytes 49152
  44.3 0.4 copy-done
  44.7 0.7 %copy.16 = f32[6,16,16,8]{2,3,1,0:T(8,128)} copy(f32[6,16,16,8]{2,3,1,0:T(8,128)S(1)} %bitcast.22) | data formatting | bytes 98304
Async XLA Ops:
  41.3 2.3 %copy-start.1 = (f32[384,16]{1,0:T(8,128)S(1)}, f32[384,16]{1,0:T(8,128)}, u32[]{:S(2)}) copy-start(f32[384,16]{1,0:T(8,128)} %get-tuple-element.7) | copy-start | bytes 73732
  43.6 1.1 %copy-start = (f32[768,16]{1,0:T(8,128)S(1)}, f32[768,16]{1,0:T(8,128)}, u32[]{:S(2)}) copy-start(f32[768,16]{1,0:T(8,128)} %get-tuple-element.8) | copy-start | bytes 147460

commit v3 on v2

--- a/solution.py
+++ b/solution.py
@@ -19,6 +19,7 @@
 PARTS = 19
 ROWS = 24
 FULL = 32767.0
+VMEM_LIMIT = 56 * 1024 * 1024
 NEAR = 4
 
 
@@ -428,14 +429,19 @@
 
 
 def main_kernel(*refs):
-    given, outs, refs = refs[:8], refs[8:11], refs[11:]
-    stiff_out, velocity_out, stress_out = outs
+    given, outs, refs = refs[:8], refs[8:10], refs[10:]
     held, refs = refs[:8], refs[8:]
     angles, table, seeds, even, packed, from_row, from_lane, partial = refs[:8]
     refs = refs[8:]
-    fields, arrived, first, first_in, second, second_in, stiff, load_sem = refs[:8]
-    rs_send, rs_recv, p1_send, p1_recv, p2_send, p2_recv = refs[8:14]
-    halo_refs = refs[14:]
+    fields, arrived, first, first_in, second, second_in, stiff, waves = refs[:8]
+    load_sem, out_sem = refs[8:10]
+    rs_send, rs_recv, p1_send, p1_recv, p2_send, p2_recv = refs[10:16]
+    halo_refs = refs[16:]
+    stores = [
+        pltpu.make_async_copy(stiff, outs[0], out_sem.at[0]),
+        pltpu.make_async_copy(waves.at[0:48], outs[1].at[0:48], out_sem.at[1]),
+        pltpu.make_async_copy(waves.at[48:144], outs[1].at[48:144], out_sem.at[2]),
+    ]
 
     loads = [pltpu.make_async_copy(given[i], held[i], load_sem.at[i]) for i in range(8)]
     for load in loads:
@@ -449,9 +455,11 @@
     for end in ends:
         pl.semaphore_signal(barrier, inc=1, device_id=end, device_id_type=MESH)
 
-    for i in range(5):
+    loads[0].wait()
+    loads[1].wait()
+    prepare_table(euler, crystal, angles, table, seeds, even)
+    for i in range(2, 5):
         loads[i].wait()
-    prepare_table(euler, crystal, angles, table, seeds, even)
     prepare_cells(orient, weight, cell_map, packed, from_row, from_lane)
 
     halos = [Halo(step, halo_refs, (x, y, a)) for step in range(2 * STEPS)]
@@ -563,26 +571,60 @@
     stresses = [fields[i * 16 : i * 16 + 16, :] for i in range(6)]
     stresses = new_stress(stresses, strain, stiff)
     halos[2].start(stress_parts(stresses))
-    for row in range(16):
-        turned = jnp.transpose(stiff[:, row, :], (1, 0))
-        for z in range(8):
-            stiff_out[pl.ds(row * 128 + z, 16, stride=8), :] = turned[z * 16 : z * 16 + 16, :21]
+    stores[0].start()
     factor = fields[144:160, :]
     velocities = [fields[96 + k * 16 : 112 + k * 16, :] for k in range(3)]
     velocities = new_velocity(velocities, halos[2].finish(), factor)
     halos[3].start((velocities,) * 3)
     for k in range(3):
-        for z in range(8):
-            velocity_out[pl.ds(k * 128 + z, 16, stride=8), :] = velocities[k][:, z * 16 : z * 16 + 16]
+        waves[k * 16 : k * 16 + 16, :] = velocities[k]
+    stores[1].start()
     strain = strain_rates(halos[3].finish())
     stresses = new_stress(stresses, strain, stiff)
     for k in range(6):
+        waves[48 + k * 16 : 64 + k * 16, :] = stresses[k]
+    stores[2].start()
+    for store in stores:
+        store.wait()
+
+
+def layout_kernel(
+    stiff_in, waves_in, stiff_out, velocity_out, stress_out,
+    stiff, waves, stiff_held, velocity_held, stress_held, sems, load_sems,
+):
+    loads = [
+        pltpu.make_async_copy(waves_in, waves, load_sems.at[0]),
+        pltpu.make_async_copy(stiff_in, stiff, load_sems.at[1]),
+    ]
+    for load in loads:
+        load.start()
+    loads[0].wait()
+    copies = []
+
+    def send(source, target):
+        copies.append(pltpu.make_async_copy(source, target, sems.at[len(copies)]))
+        copies[-1].start()
+
+    for z in range(8):
+        lanes = slice(z * 16, z * 16 + 16)
+        stress_held[pl.ds(z, 96, stride=8), :] = waves[48:144, lanes]
+        velocity_held[pl.ds(z, 48, stride=8), :] = waves[0:48, lanes]
+    send(stress_held, stress_out)
+    send(velocity_held, velocity_out)
+    loads[1].wait()
+    for row in range(16):
+        turned = jnp.transpose(stiff[:, row, :], (1, 0))
         for z in range(8):
-            stress_out[pl.ds(k * 128 + z, 16, stride=8), :] = stresses[k][:, z * 16 : z * 16 + 16]
+            stiff_held[pl.ds(row * 128 + z, 16, stride=8), :] = turned[z * 16 : z * 16 + 16, :21]
+        if row % 4 == 3:
+            rows = pl.ds((row - 3) * 128, 512)
+            send(stiff_held.at[rows, :], stiff_out.at[rows, :])
+    for copy in copies:
+        copy.wait()
 
 
 def on_device(euler_table, crystal, orient, weight, cell_map, density, velocity, stress):
-    anywhere, vmem = pl.BlockSpec(memory_space=pl.ANY), pl.BlockSpec(memory_space=pltpu.VMEM)
+    anywhere = pl.BlockSpec(memory_space=pl.ANY)
     operands = (
         euler_table,
         crystal,
@@ -612,9 +654,11 @@
         pltpu.VMEM((16, ROWS, 128), F32),
         pltpu.VMEM((8, 2, ROWS, 128), F32),
         pltpu.VMEM((8, 2, ROWS, 128), F32),
-        pltpu.VMEM((21, 16, 128), F32),
     ]
-    for count in (8, 2, 2, 15, 15, 7, 7):
+    small = (jax.ShapeDtypeStruct((21, 16, 128), F32), jax.ShapeDtypeStruct((144, 128), F32))
+    small_held = [pltpu.VMEM(array.shape, F32) for array in small]
+    scratch += small_held
+    for count in (8, 3, 2, 2, 15, 15, 7, 7):
         scratch.append(pltpu.SemaphoreType.DMA((count,)))
     steps = 2 * STEPS
     scratch += [
@@ -629,21 +673,29 @@
         pltpu.SemaphoreType.DMA((steps, 5)),
         pltpu.SemaphoreType.DMA((steps, 5)),
     ]
-    stiffness, velocity, stress = pl.pallas_call(
+    found = pl.pallas_call(
         main_kernel,
-        out_shape=(
-            jax.ShapeDtypeStruct((2048, 21), F32),
-            jax.ShapeDtypeStruct((384, 16), F32),
-            jax.ShapeDtypeStruct((768, 16), F32),
-        ),
+        out_shape=small,
         in_specs=[anywhere] * 8,
-        out_specs=(vmem, vmem, vmem),
+        out_specs=(anywhere, anywhere),
         scratch_shapes=scratch,
         compiler_params=pltpu.CompilerParams(
-            collective_id=0, has_side_effects=True, vmem_limit_bytes=56 * 1024 * 1024
+            collective_id=0, has_side_effects=True, vmem_limit_bytes=VMEM_LIMIT
         ),
         name="relay_and_steps",
     )(*operands)
+    shapes = ((2048, 21), (384, 16), (768, 16))
+    stiffness, velocity, stress = pl.pallas_call(
+        layout_kernel,
+        out_shape=tuple(jax.ShapeDtypeStruct(shape, F32) for shape in shapes),
+        in_specs=[anywhere, anywhere],
+        out_specs=(anywhere,) * 3,
+        scratch_shapes=small_held
+        + [pltpu.VMEM(shape, F32) for shape in shapes]
+        + [pltpu.SemaphoreType.DMA((6,)), pltpu.SemaphoreType.DMA((2,))],
+        compiler_params=pltpu.CompilerParams(vmem_limit_bytes=VMEM_LIMIT),
+        name="layouts",
+    )(*found)
     return (
         stiffness.reshape(16, 16, 8, 21).transpose(3, 0, 1, 2),
         velocity.reshape(3, 16, 8, 16).transpose(0, 1, 3, 2),

time: 45.8 us -> 43.3 us (0.945)
  local copies, waits for them, and re-layouts: 4.15 us -> 0 us
  Pallas kernels: 40.6 us -> 42.3 us
    unnamed x7 -> x0, local copies, waits for them, and re-layouts: 4.15 us -> none
    pallas_call x1 -> x2, Pallas kernels: 40.6 us -> 42.3 us  [the longest x1 40 us: on_device(): pl.pallas_call(main_kernel, out_shape=small, in_specs=[anywhere] * 8, out...]
where the time goes in v3:
time: 43.3 us; the launch traced here: 42.9 us
  Pallas kernels  42.3 us (98%)
  between operations  0.64 us (1%)
    pallas_call x1, Pallas kernels, on_device(): pl.pallas_call(main_kernel, out_shape=small, in_specs=[anywhere] * 8, out...  40 us
    pallas_call x1, Pallas kernels, on_device(): pl.pallas_call(layout_kernel, out_shape=tuple((jax.ShapeDtypeStruct(shape...  2.3 us

profile of v3, /device:TPU:32, one launch (start us, length us, event | category | flops | bytes accessed | tf_op | source)
XLA Modules:
  0.0 42.9 jit_solution(3842089295683354901)
XLA Ops:
  0.6 40.0 %relay_and_steps.1 = (f32[21,16,128]{2,1,0:T(8,128)}, f32[144,128]{1,0:T(8,128)}) custom-call(f32[3,2048]{1,0:T(4,128)} %refs_0_.1, f32[21]{0:T(128)} %refs_1_.1, s32[512,128]{1,0:T(8,128)} %bitcast.22, bf16[16,4096]{1,0:T(8,128)(2,1)} %bitcast.24, s32[32,128]{1,0:T(8,128)} %bitcast.26, f32[128,16]{1,0:T(8,128)} %bitcast.25, f32[384,16]{1,0:T(8,128)} %bitcast.23, ...), custom_call_target="tpu_custom_call" | custom-call | tf_op jit(solution)/shard_map/relay_and_steps/pallas_call | solution.py:676
  40.6 2.3 %layouts.1 = (f32[2048,21]{1,0:T(8,128)}, f32[384,16]{1,0:T(8,128)}, f32[768,16]{1,0:T(8,128)}) custom-call(f32[21,16,128]{2,1,0:T(8,128)} %get-tuple-element.8.stiff_in, f32[144,128]{1,0:T(8,128)} %get-tuple-element.9.waves_in), custom_call_target="tpu_custom_call" | custom-call | tf_op jit(solution)/shard_map/layouts/pallas_call | solution.py:688

commit v4 on v3

--- a/solution.py
+++ b/solution.py
@@ -18,7 +18,7 @@
 GRAINS = 16
 PARTS = 19
 ROWS = 24
-FULL = 32767.0
+STEP = 1 << 19
 VMEM_LIMIT = 56 * 1024 * 1024
 NEAR = 4
 
@@ -170,18 +170,31 @@
     return lax.broadcasted_iota(I32, (rows, 128), 0)
 
 
-def pair_word(first, second):
-    low = jnp.floor(second * FULL + 0.5)
-    high = jnp.floor(first * FULL - low * (1.0 / 65536.0) + 0.5).astype(I32)
-    return high * 65536 + low.astype(I32)
+def angle_field(angle):
+    cos, sin = jnp.cos(angle), jnp.sin(angle)
+    back = cos < 0.0
+    tangent = jnp.where(back, -sin, sin) / (1.0 + jnp.abs(cos))
+    whole = jnp.floor(tangent * STEP + 0.5).astype(I32)
+    return jnp.clip(whole, -STEP, STEP - 1) * 2 + back.astype(I32)
+
+
+def cos_sin(field):
+    tangent = field.astype(F32) * (0.5 / STEP)
+    square = tangent * tangent
+    below = 1.0 + square
+    rough = pl.reciprocal(below, approx=True)
+    fine = rough * (2.0 - below * rough)
+    fine = jnp.where((field & 1) == 1, -fine, fine)
+    return (1.0 - square) * fine, (tangent + tangent) * fine
 
 
 def prepare_table(euler, crystal, angles, table, seeds, even):
     for j in range(16):
         angles[pl.ds(j, 3, stride=16), :] = euler[:, j * 128 : (j + 1) * 128]
-    for k in range(3):
-        angle = angles[k * 16 : k * 16 + 16, :]
-        table[k * 16 : k * 16 + 16, :] = pair_word(jnp.cos(angle), jnp.sin(angle))
+    turns = [angle_field(angles[k * 16 : k * 16 + 16, :]) for k in range(3)]
+    last = turns[2] + 2 * STEP
+    table[0:16, :] = turns[0] * 2048 + (last >> 11)
+    table[16:32, :] = turns[1] * 2048 + (last & 2047)
     values = [jnp.full((8, 128), crystal[i], F32) for i in range(21)]
     for i in range(PARTS):
         seeds[i] = sparse(TO_PARTS[i], values)
@@ -248,20 +261,17 @@
                 ],
                 bits,
             )
-            for k in range(3)
+            for k in range(2)
         ]
 
     def absorb(grain, carry):
-        word, pairs, sums = carry[0], carry[1:4], carry[4:]
-        coming = carry[0 + 4 + PARTS + 1]
-        sums = sums[: PARTS + 1]
+        word, coming, one, two = carry[:4]
+        sums = carry[4:]
         after = fetch(jnp.minimum(grain + 2, GRAINS - 1))
-        coming_pairs = angles_of(coming)
+        coming_pair = angles_of(coming)
         mass = (word & 4095).astype(F32)
-        unit = 1.0 / (FULL * 65536.0)
-        turns = [
-            multiples(pair.astype(F32) * unit, (pair << 16).astype(F32) * unit) for pair in pairs
-        ]
+        fields = (one >> 11, two >> 11, ((one & 1023) << 11) + (two & 2047) - 2 * STEP)
+        turns = [multiples(*cos_sin(field)) for field in fields]
         cos, sin = turns[2]
         cos = [mass] + [mass * value for value in cos[1:]]
         sin = [None] + [mass * value for value in sin[1:]]
@@ -271,12 +281,12 @@
         parts = quarter_turn(parts, QUARTER)
         parts = about_z(parts, *turns[0])
         out = [old + new for old, new in zip(sums, parts)] + [sums[PARTS] + mass]
-        return (coming, *coming_pairs, *out, after)
+        return (coming, after, *coming_pair, *out)
 
     zero = jnp.zeros((8, 128), F32)
     first, second = fetch(0), fetch(1)
-    carry = (first, *angles_of(first)) + (zero,) * (PARTS + 1) + (second,)
-    return lax.fori_loop(0, GRAINS, absorb, carry)[4 : 4 + PARTS + 1]
+    carry = (first, second, *angles_of(first)) + (zero,) * (PARTS + 1)
+    return lax.fori_loop(0, GRAINS, absorb, carry)[4:]
 
 
 def block_swap(block, regroup):
@@ -641,7 +651,7 @@
     ]
     scratch += [
         pltpu.VMEM((48, 128), F32),
-        pltpu.VMEM((48, 128), I32),
+        pltpu.VMEM((32, 128), I32),
         pltpu.VMEM((PARTS, 8, 128), F32),
         pltpu.VMEM((21, 8, 128), F32),
         pltpu.VMEM((512, 128), I32),

time: 43.3 us -> 42.2 us (0.975)
  Pallas kernels: 42.3 us -> 41.4 us
    pallas_call x1, Pallas kernels: 40 us -> 39.1 us  [on_device(): pl.pallas_call(main_kernel, out_shape=small, in_specs=[anywhere] * 8, out...]
where the time goes in v4:
time: 42.2 us; the launch traced here: 42 us
  Pallas kernels  41.4 us (98%)
  between operations  0.64 us (2%)
    pallas_call x1, Pallas kernels, on_device(): pl.pallas_call(main_kernel, out_shape=small, in_specs=[anywhere] * 8, out...  39.1 us
    pallas_call x1, Pallas kernels, on_device(): pl.pallas_call(layout_kernel, out_shape=tuple((jax.ShapeDtypeStruct(shape...  2.3 us

profile of v4, /device:TPU:32, one launch (start us, length us, event | category | flops | bytes accessed | tf_op | source)
XLA Modules:
  0.0 42.0 jit_solution(15666955365149760339)
XLA Ops:
  0.6 39.1 %relay_and_steps.1 = (f32[21,16,128]{2,1,0:T(8,128)}, f32[144,128]{1,0:T(8,128)}) custom-call(f32[3,2048]{1,0:T(4,128)} %refs_0_.1, f32[21]{0:T(128)} %refs_1_.1, s32[512,128]{1,0:T(8,128)} %bitcast.22, bf16[16,4096]{1,0:T(8,128)(2,1)} %bitcast.24, s32[32,128]{1,0:T(8,128)} %bitcast.26, f32[128,16]{1,0:T(8,128)} %bitcast.25, f32[384,16]{1,0:T(8,128)} %bitcast.23, ...), custom_call_target="tpu_custom_call" | custom-call | tf_op jit(solution)/shard_map/relay_and_steps/pallas_call | solution.py:686
  39.7 2.3 %layouts.1 = (f32[2048,21]{1,0:T(8,128)}, f32[384,16]{1,0:T(8,128)}, f32[768,16]{1,0:T(8,128)}) custom-call(f32[21,16,128]{2,1,0:T(8,128)} %get-tuple-element.8.stiff_in, f32[144,128]{1,0:T(8,128)} %get-tuple-element.9.waves_in), custom_call_target="tpu_custom_call" | custom-call | tf_op jit(solution)/shard_map/layouts/pallas_call | solution.py:698

commit v5 on v4

--- a/solution.py
+++ b/solution.py
@@ -19,7 +19,9 @@
 PARTS = 19
 ROWS = 24
 STEP = 1 << 19
+LEAST = 76
 VMEM_LIMIT = 56 * 1024 * 1024
+FIRST = 5
 NEAR = 4
 
 
@@ -207,7 +209,14 @@
     for j in range(32):
         mass = (weight[:, j * 128 : (j + 1) * 128].astype(F32) * 2048.0).astype(I32)
         chosen = orient[pl.ds(j, GRAINS, stride=32), :]
-        packed[pl.ds(j, GRAINS, stride=32), :] = chosen * 4096 + mass
+        power = ordered_sum([(mass >= bound).astype(I32) for bound in (256, 512, 1024, 2048)])
+        code = power * 128 + (mass >> power) - (128 + LEAST)
+        packed[pl.ds(j, GRAINS, stride=32), :] = chosen * 512 + code
+    for quad in range(GRAINS // 4):
+        four = [packed[(4 * quad + k) * 32 : (4 * quad + k) * 32 + 32, :] for k in range(4)]
+        words = (four[0] + ((four[3] & 4095) << 20), four[1] + ((four[3] >> 12) << 20), four[2])
+        for k in range(3):
+            packed[(3 * quad + k) * 32 : (3 * quad + k) * 32 + 32, :] = words[k]
     me_x, me_a = lax.axis_index("gx"), lax.axis_index("ga")
     slot = cell_map[...]
     depth = slot & 15
@@ -234,42 +243,46 @@
     from_lane[...] = found[32:]
 
 
-def grain_sums(table, seeds, packed, from_row, from_lane, start):
-    lane = from_lane[start : start + 8, :]
-    row = from_row[start : start + 8, :]
-    row_bits = [((row >> bit) & 1) == 1 for bit in range(5)]
-
-    def fetch(grain):
-        return tree(
-            [
-                lane_pick(jnp.broadcast_to(packed[pl.ds(grain * 32 + j, 1), :], (8, 128)), lane)
-                for j in range(32)
-            ],
-            row_bits,
-        )
-
-    def angles_of(word):
-        spot = (word >> 12) & 127
-        bits = [((word >> (19 + bit)) & 1) == 1 for bit in range(4)]
+def grain_sums(table, seeds, packed, from_row, from_lane, block, carry=None):
+    quads = GRAINS // 4
+
+    def fetch(step):
+        step = jnp.minimum(step, 4 * quads - 1)
+        first = lax.rem(step, quads) * 96
+        rows = pl.ds(pl.multiple_of(lax.div(step, quads) * 8, 8), 8)
+        lane, row = from_lane[rows, :], from_row[rows, :]
+        bits = [((row >> bit) & 1) == 1 for bit in range(5)]
         return [
             tree(
                 [
                     lane_pick(
-                        jnp.broadcast_to(table[k * 16 + h : k * 16 + h + 1, :], (8, 128)), spot
+                        jnp.broadcast_to(packed[pl.ds(first + k * 32 + j, 1), :], (8, 128)), lane
                     )
-                    for h in range(16)
+                    for j in range(32)
                 ],
                 bits,
             )
-            for k in range(2)
+            for k in range(3)
         ]
 
-    def absorb(grain, carry):
-        word, coming, one, two = carry[:4]
-        sums = carry[4:]
-        after = fetch(jnp.minimum(grain + 2, GRAINS - 1))
-        coming_pair = angles_of(coming)
-        mass = (word & 4095).astype(F32)
+    def look_up(words):
+        low = (1 << 20) - 1
+        last = ((words[0] >> 20) & 4095) + ((words[1] >> 20) << 12)
+        found = []
+        for word in (words[0] & low, words[1] & low, words[2], last):
+            spot = (word >> 9) & 127
+            bits = [((word >> (16 + bit)) & 1) == 1 for bit in range(4)]
+            found.append(word)
+            for k in range(2):
+                rows = [table[k * 16 + h : k * 16 + h + 1, :] for h in range(16)]
+                found.append(
+                    tree([lane_pick(jnp.broadcast_to(r, (8, 128)), spot) for r in rows], bits)
+                )
+        return found
+
+    def add(word, one, two, sums):
+        code = (word & 511) + LEAST
+        mass = ((128 + (code & 127)) << (code >> 7)).astype(F32)
         fields = (one >> 11, two >> 11, ((one & 1023) << 11) + (two & 2047) - 2 * STEP)
         turns = [multiples(*cos_sin(field)) for field in fields]
         cos, sin = turns[2]
@@ -280,13 +293,22 @@
         parts = about_z(parts, *turns[1])
         parts = quarter_turn(parts, QUARTER)
         parts = about_z(parts, *turns[0])
-        out = [old + new for old, new in zip(sums, parts)] + [sums[PARTS] + mass]
-        return (coming, after, *coming_pair, *out)
-
-    zero = jnp.zeros((8, 128), F32)
-    first, second = fetch(0), fetch(1)
-    carry = (first, second, *angles_of(first)) + (zero,) * (PARTS + 1)
-    return lax.fori_loop(0, GRAINS, absorb, carry)[4:]
+        return [old + new for old, new in zip(sums, parts)] + [sums[PARTS] + mass]
+
+    def absorb(step, carry):
+        words, found, sums = carry[:3], carry[3:15], carry[15:]
+        after = fetch(step + 2)
+        coming = look_up(words)
+        for k in range(4):
+            sums = add(*found[3 * k : 3 * k + 3], sums)
+        return (*after, *coming, *sums)
+
+    if carry is None:
+        carry = (*fetch(jnp.int32(1)), *look_up(fetch(jnp.int32(0))))
+    sums = (jnp.zeros((8, 128), F32),) * (PARTS + 1)
+    begin = block * quads
+    out = lax.fori_loop(begin, begin + quads, absorb, (*carry, *sums))
+    return out[15:], out[:15]
 
 
 def block_swap(block, regroup):
@@ -359,48 +381,60 @@
             for n, ((source, target), end) in enumerate(zip(pairs, ends))
         ]
 
-    def start(self, along):
-        self.fields = along
-        fx, fy, fz = along
+    def start_y(self, fields):
+        self.along_y = fields
         i = self.step
         quarter = (lane_iota(16) & 15) >> 2
-        for k in range(3):
-            self.xs[i, k] = fx[k]
-        self.copies[0].start()
-        self.copies[1].start()
         for side, offset in ((0, 128 - 12), (1, 0)):
             rolled = [
-                pltpu.roll(fy[k], (offset + 4 * k) % 128, 1) if (offset + 4 * k) % 128 else fy[k]
+                pltpu.roll(fields[k], (offset + 4 * k) % 128, 1) if offset + 4 * k else fields[k]
                 for k in range(3)
             ]
             self.ys[i, side] = jnp.where(
                 quarter == 0, rolled[0], jnp.where(quarter == 1, rolled[1], rolled[2])
             )
             self.copies[2 + side].start()
+
+    def start_x(self, fields):
+        self.along_x = fields
         for k in range(3):
-            self.zs[i, k] = fz[k]
+            self.xs[self.step, k] = fields[k]
+        self.copies[0].start()
+        self.copies[1].start()
+
+    def start_z(self, fields):
+        self.along_z = fields
+        for k in range(3):
+            self.zs[self.step, k] = fields[k]
         self.copies[4].start()
+
+    def start(self, along):
+        fx, fy, fz = along
+        self.start_y(fy)
+        self.start_x(fx)
+        self.start_z(fz)
 
     def finish(self):
         x, y, a = self.me
-        fx, fy, fz = self.fields
         i = self.step
-        for copy in self.copies:
-            copy.wait()
-        for k in range(3):
-            self.xb[k, 0:8, :] = jnp.where(x > 0, self.xl[i, k], 0.0)
-            self.xb[k, 8:24, :] = fx[k]
-            self.xb[k, 24:32, :] = jnp.where(x < GX - 1, self.xr[i, k], 0.0)
-        dx = [along_x(self.xb.at[k]) for k in range(3)]
-        low = jnp.where(y > 0, self.yr[i, 0], 0.0)
-        high = jnp.where(y < GY - 1, self.yr[i, 1], 0.0)
-        dy = [along_y(fy[k], k, low, high) for k in range(3)]
+        self.copies[4].wait()
         dz = []
         for k in range(3):
             other = self.zr[i, k]
-            dz.append(
-                along_z(fz[k], jnp.where(a > 0, other, 0.0), jnp.where(a == 0, other, 0.0))
-            )
+            low, high = jnp.where(a > 0, other, 0.0), jnp.where(a == 0, other, 0.0)
+            dz.append(along_z(self.along_z[k], low, high))
+        self.copies[0].wait()
+        self.copies[1].wait()
+        for k in range(3):
+            self.xb[k, 0:8, :] = jnp.where(x > 0, self.xl[i, k], 0.0)
+            self.xb[k, 8:24, :] = self.along_x[k]
+            self.xb[k, 24:32, :] = jnp.where(x < GX - 1, self.xr[i, k], 0.0)
+        dx = [along_x(self.xb.at[k]) for k in range(3)]
+        self.copies[2].wait()
+        self.copies[3].wait()
+        low = jnp.where(y > 0, self.yr[i, 0], 0.0)
+        high = jnp.where(y < GY - 1, self.yr[i, 1], 0.0)
+        dy = [along_y(self.along_y[k], k, low, high) for k in range(3)]
         return dx, dy, dz
 
 
@@ -414,13 +448,13 @@
     return [dx[0], dy[1], dz[2], dy[2] + dz[1], dx[2] + dz[0], dx[1] + dy[0]]
 
 
+def new_component(stress, strain, stiffness, row):
+    change = ordered_sum([stiffness[upper(row, col)] * strain[col] for col in range(6)])
+    return stress[row] + time_step * change
+
+
 def new_stress(stress, strain, stiffness):
-    return [
-        stress[row]
-        + time_step
-        * ordered_sum([stiffness[upper(row, col)] * strain[col] for col in range(6)])
-        for row in range(6)
-    ]
+    return [new_component(stress, strain, stiffness, row) for row in range(6)]
 
 
 def stress_parts(stress):
@@ -484,29 +518,35 @@
         )
         for i in range(2)
     ]
+    def slot_of(d):
+        return (GX - d - FIRST) % GX
+
     to_brick = {}
     for row in range(16):
         d = (row + NEAR) % GX
         if d:
             to_brick[row] = pltpu.make_async_remote_copy(
                 src_ref=first.at[row, 0:PARTS],
-                dst_ref=first_in.at[x, 0:PARTS],
+                dst_ref=first_in.at[slot_of(d), 0:PARTS],
                 send_sem=p1_send.at[d - 1],
                 recv_sem=p1_recv.at[d - 1],
                 device_id=((x + d) % GX, y, a),
                 device_id_type=MESH,
             )
 
-    def sums_of(start):
-        return grain_sums(table, seeds, packed, from_row, from_lane, start)
+    carry = [None]
+
+    def sums_of(block):
+        sums, carry[0] = grain_sums(table, seeds, packed, from_row, from_lane, block, carry[0])
+        return sums
 
     def other_half(i):
-        sums = sums_of(i * 8)
+        sums = sums_of(i)
         for c in range(PARTS + 1):
             partial[i * 8 : i * 8 + 8, c, :] = sums[c]
 
     def own_half(i):
-        sums = sums_of(16 + i * 8)
+        sums = sums_of(2 + i)
         half[i].wait()
         rows = slice(i * 8, i * 8 + 8)
         gain = 1.0 / (sums[PARTS] + arrived[rows, PARTS, :])
@@ -539,48 +579,62 @@
     fields[144:160, :] = factor
     halos[1].start((velocities,) * 3)
     own_half(1)
+
+    to_y = []
+
+    def forward(g):
+        for c in range(PARTS):
+            block = first_in[g * 8 : g * 8 + 8, c, :]
+            second[:, g, c, :] = block_swap(block, False)
+        for d in range(1, GY):
+            target = (y + d) % GY
+            copy = pltpu.make_async_remote_copy(
+                src_ref=second.at[target, g, 0:PARTS],
+                dst_ref=second_in.at[y, g, 0:PARTS],
+                send_sem=p2_send.at[g * (GY - 1) + d - 1],
+                recv_sem=p2_recv.at[g * (GY - 1) + d - 1],
+                device_id=(x, target, a),
+                device_id_type=MESH,
+            )
+            copy.start()
+            to_y.append(copy)
+        second_in[y, g, 0:PARTS, :] = second[y, g, 0:PARTS, :]
+
+    for row in range(8):
+        to_brick[row].wait()
+    forward(0)
     velocities = [fields[96 + k * 16 : 112 + k * 16, :] for k in range(3)]
-    halos[1].fields = (velocities,) * 3
+    halos[1].along_x = halos[1].along_y = halos[1].along_z = velocities
     strain = strain_rates(halos[1].finish())
     for i in range(6):
         fields[160 + i * 16 : 176 + i * 16, :] = strain[i]
-    first_in[x, 0:PARTS, :] = first[GX - NEAR, 0:PARTS, :]
-    for copy in to_brick.values():
-        copy.wait()
-
-    for p in range(2):
-        for c in range(PARTS):
-            block = first_in[p * 8 : p * 8 + 8, c, :]
-            second[:, p, c, :] = block_swap(block, False)
-    to_y = []
-    for d in range(1, GY):
-        target = (y + d) % GY
-        copy = pltpu.make_async_remote_copy(
-            src_ref=second.at[target, :, 0:PARTS],
-            dst_ref=second_in.at[y, :, 0:PARTS],
-            send_sem=p2_send.at[d - 1],
-            recv_sem=p2_recv.at[d - 1],
-            device_id=(x, target, a),
-            device_id_type=MESH,
-        )
-        copy.start()
-        to_y.append(copy)
-    for p in range(2):
-        second_in[y, p, 0:PARTS, :] = second[y, p, 0:PARTS, :]
+    first_in[slot_of(0), 0:PARTS, :] = first[GX - NEAR, 0:PARTS, :]
+    for row in range(8, 16):
+        if row in to_brick:
+            to_brick[row].wait()
+    forward(1)
     for copy in to_y:
         copy.wait()
     parts = []
     for c in range(PARTS):
-        parts.append(
-            jnp.concatenate([block_swap(second_in[:, p, c, :], True) for p in range(2)], axis=0)
-        )
+        rows = [block_swap(second_in[:, g, c, :], True) for g in range(2)]
+        parts.append(pltpu.roll(jnp.concatenate(rows, axis=0), (x + FIRST) % GX, 0))
     for i, entry in enumerate(entries_of(parts, even)):
         stiff[i] = entry
 
     strain = [fields[160 + i * 16 : 176 + i * 16, :] for i in range(6)]
     stresses = [fields[i * 16 : i * 16 + 16, :] for i in range(6)]
-    stresses = new_stress(stresses, strain, stiff)
-    halos[2].start(stress_parts(stresses))
+    fresh = {}
+    for which, begin in (
+        (STRESS_Y, halos[2].start_y),
+        (STRESS_X, halos[2].start_x),
+        (STRESS_Z, halos[2].start_z),
+    ):
+        for row in which:
+            if row not in fresh:
+                fresh[row] = new_component(stresses, strain, stiff, row)
+        begin([fresh[row] for row in which])
+    stresses = [fresh[row] for row in range(6)]
     stores[0].start()
     factor = fields[144:160, :]
     velocities = [fields[96 + k * 16 : 112 + k * 16, :] for k in range(3)]
@@ -668,7 +722,7 @@
     small = (jax.ShapeDtypeStruct((21, 16, 128), F32), jax.ShapeDtypeStruct((144, 128), F32))
     small_held = [pltpu.VMEM(array.shape, F32) for array in small]
     scratch += small_held
-    for count in (8, 3, 2, 2, 15, 15, 7, 7):
+    for count in (8, 3, 2, 2, 15, 15, 14, 14):
         scratch.append(pltpu.SemaphoreType.DMA((count,)))
     steps = 2 * STEPS
     scratch += [

time: 42.2 us -> 40.8 us (0.967); the launches traced: 42 us -> 40 us
  Pallas kernels: 41.4 us -> 39.4 us
    pallas_call x1, Pallas kernels: 39.1 us -> 37.1 us  [on_device(): pl.pallas_call(main_kernel, out_shape=small, in_specs=[anywhere] * 8, out...]
where the time goes in v5:
time: 40.8 us; the launch traced here: 40 us
  Pallas kernels  39.4 us (97%)
  between operations  0.64 us (2%)
    pallas_call x1, Pallas kernels, on_device(): pl.pallas_call(main_kernel, out_shape=small, in_specs=[anywhere] * 8, out...  37.1 us
    pallas_call x1, Pallas kernels, on_device(): pl.pallas_call(layout_kernel, out_shape=tuple((jax.ShapeDtypeStruct(shape...  2.3 us

profile of v5, /device:TPU:32, one launch (start us, length us, event | category | flops | bytes accessed | tf_op | source)
XLA Modules:
  0.0 40.0 jit_solution(13427488649885344784)
XLA Ops:
  0.6 37.1 %relay_and_steps.1 = (f32[21,16,128]{2,1,0:T(8,128)}, f32[144,128]{1,0:T(8,128)}) custom-call(f32[3,2048]{1,0:T(4,128)} %refs_0_.1, f32[21]{0:T(128)} %refs_1_.1, s32[512,128]{1,0:T(8,128)} %bitcast.22, bf16[16,4096]{1,0:T(8,128)(2,1)} %bitcast.24, s32[32,128]{1,0:T(8,128)} %bitcast.26, f32[128,16]{1,0:T(8,128)} %bitcast.25, f32[384,16]{1,0:T(8,128)} %bitcast.23, ...), custom_call_target="tpu_custom_call" | custom-call | tf_op jit(solution)/shard_map/relay_and_steps/pallas_call | solution.py:740
  37.7 2.3 %layouts.1 = (f32[2048,21]{1,0:T(8,128)}, f32[384,16]{1,0:T(8,128)}, f32[768,16]{1,0:T(8,128)}) custom-call(f32[21,16,128]{2,1,0:T(8,128)} %get-tuple-element.8.stiff_in, f32[144,128]{1,0:T(8,128)} %get-tuple-element.9.waves_in), custom_call_target="tpu_custom_call" | custom-call | tf_op jit(solution)/shard_map/layouts/pallas_call | solution.py:752

commit v6 on v5

--- a/solution.py
+++ b/solution.py
@@ -493,7 +493,7 @@
     euler, crystal, orient, weight, cell_map, density, velocity, stress = held
     x, y, a = lax.axis_index("gx"), lax.axis_index("gy"), lax.axis_index("ga")
     barrier = pltpu.get_barrier_semaphore()
-    ends = [((x + d) % GX, y, a) for d in range(1, GX)]
+    ends = [((x + d) % GX, y, a) for d in sorted(range(1, GX), key=lambda d: -min(d, GX - d))]
     ends += [(x, (y + d) % GY, a) for d in range(1, GY)]
     ends += [(x, y, 1 - a)]
     for end in ends:
@@ -552,7 +552,7 @@
         gain = 1.0 / (sums[PARTS] + arrived[rows, PARTS, :])
         for c in range(PARTS):
             first[rows, c, :] = (sums[c] + arrived[rows, c, :]) * gain
-        for row in range(i * 8, i * 8 + 8):
+        for row in (4, 3, 5, 2, 6, 1, 7, 0) if i == 0 else (8, 9, 15, 10, 14, 11, 13, 12):
             if row in to_brick:
                 to_brick[row].start()
 
@@ -586,7 +586,7 @@
         for c in range(PARTS):
             block = first_in[g * 8 : g * 8 + 8, c, :]
             second[:, g, c, :] = block_swap(block, False)
-        for d in range(1, GY):
+        for d in (6, 2, 4, 5, 3, 7, 1):
             target = (y + d) % GY
             copy = pltpu.make_async_remote_copy(
                 src_ref=second.at[target, g, 0:PARTS],

time: 40.8 us -> 40.5 us (level); the launches traced: 40 us -> 40.4 us
  no operation moved by 1% of the time
where the time goes in v6:
time: 40.5 us; the launch traced here: 40.4 us
  Pallas kernels  39.7 us (98%)
  between operations  0.64 us (2%)
    pallas_call x1, Pallas kernels, on_device(): pl.pallas_call(main_kernel, out_shape=small, in_specs=[anywhere] * 8, out...  37.4 us
    pallas_call x1, Pallas kernels, on_device(): pl.pallas_call(layout_kernel, out_shape=tuple((jax.ShapeDtypeStruct(shape...  2.3 us

profile of v6, /device:TPU:32, one launch (start us, length us, event | category | flops | bytes accessed | tf_op | source)
XLA Modules:
  0.0 40.4 jit_solution(1686127531971306883)
XLA Ops:
  0.6 37.4 %relay_and_steps.1 = (f32[21,16,128]{2,1,0:T(8,128)}, f32[144,128]{1,0:T(8,128)}) custom-call(f32[3,2048]{1,0:T(4,128)} %refs_0_.1, f32[21]{0:T(128)} %refs_1_.1, s32[512,128]{1,0:T(8,128)} %bitcast.22, bf16[16,4096]{1,0:T(8,128)(2,1)} %bitcast.24, s32[32,128]{1,0:T(8,128)} %bitcast.26, f32[128,16]{1,0:T(8,128)} %bitcast.25, f32[384,16]{1,0:T(8,128)} %bitcast.23, ...), custom_call_target="tpu_custom_call" | custom-call | tf_op jit(solution)/shard_map/relay_and_steps/pallas_call | solution.py:740
  38.0 2.3 %layouts.1 = (f32[2048,21]{1,0:T(8,128)}, f32[384,16]{1,0:T(8,128)}, f32[768,16]{1,0:T(8,128)}) custom-call(f32[21,16,128]{2,1,0:T(8,128)} %get-tuple-element.8.stiff_in, f32[144,128]{1,0:T(8,128)} %get-tuple-element.9.waves_in), custom_call_target="tpu_custom_call" | custom-call | tf_op jit(solution)/shard_map/layouts/pallas_call | solution.py:752
